TPU v7x, 256 devices: a whole 4x4x8 slice. The times are simulated.
256 devices in a mesh: req: 8 (over y, core), exp: 32 (over z, x).
Axes of the slice: x: 4, y: 4, z: 8, core: 2. Of those that a mesh axis runs over, the one named last changes fastest.
Arguments:
- latent_cache: bfloat16 [2048, 36864], P(('req', 'exp')), may hold values from -6 to 6
- old_slot: int32 [2048], P(('req', 'exp')), may hold values from 0 to 2047, as said below
- lengths: int32 [2048], P(('req', 'exp')), may hold values from 2 to 63
- new_latent: bfloat16 [2048, 576], P(('req', 'exp')), may hold values from -6 to 6
- queries: bfloat16 [2048, 36864], P(('req', 'exp')), may hold values from -110 to 110
- hidden: bfloat16 [2048, 7168], P(('req', 'exp')), may hold values from -6 to 6
- expert_ids: int32 [2048, 8], P(('req', 'exp')), may hold values from 0 to 31, all different within a row; in each aligned block of 8 rows (0 to 7, 8 to 15, ...) at most 3 rows name the same one
- expert_gates: float32 [2048, 8], P(('req', 'exp')), may hold values from 0.05 to 0.6
- gate_weight: bfloat16 [32, 7168, 1024], P('exp', 'req'), may hold values from -0.0625 to 0.0625
- up_weight: bfloat16 [32, 7168, 1024], P('exp', 'req'), may hold values from -0.0625 to 0.0625
- down_weight: bfloat16 [32, 1024, 7168], P('exp', None, 'req'), may hold values from -0.1875 to 0.1875
Outputs:
- cache_out: bfloat16 [2048, 36864], P(('req', 'exp'))
- attention: bfloat16 [2048, 32768], P(('req', 'exp'))
- moe_out: bfloat16 [2048, 7168], P(('req', 'exp'))
Inputs may be any that keep to these rules, and one draw needn't show every extreme that they name: A permutation: new row j takes the request of old row old_slot[j], which lies on the same index of exp; every device hands exactly 1 of its rows to each index of req. `expert_ids`: in the rows of one device no expert is named more than 3 times; every expert is named by some row.
All inputs are finite; a program needn't handle non-finite values.
Results may differ from a plain program's by a relative error of at most 0.029.
Values may be sent and summed in bfloat16 or wider, within the bound.
No kernel may reach another device: no remote copies, remote signals or barrier semaphores. Data moves between devices by JAX's collectives and lax.ppermute only.
A program may use at most 64 MiB of HBM per device.

v0:
```python
import functools

import jax
import jax.numpy as jnp
from jax import lax
from jax.experimental import pallas as pl
from jax.experimental.pallas import tpu as pltpu
from jax.sharding import PartitionSpec as P

LAT = 512
CAP = 3
CORES = 2
NOTE = 128

score_scale = 0.07216878364870323

VMEM = pl.BlockSpec(memory_space=pltpu.VMEM)
SMEM = pl.BlockSpec(memory_space=pltpu.SMEM)
PARAMS = pltpu.CompilerParams(vmem_limit_bytes=40 * 1024 * 1024)
BF = jnp.bfloat16
F32 = jnp.float32


def iota(shape, axis):
    return lax.broadcasted_iota(jnp.int32, shape, axis)


def dot(a, b, contract=((1,), (0,))):
    return lax.dot_general(a, b, (contract, ((), ())), preferred_element_type=F32)


def shape_of(shape, dtype=BF):
    return jax.ShapeDtypeStruct(shape, dtype)


def announce_kernel(column_span, slot_ref, hidden_ref, ids_ref, gates_ref, out_ref):
    peers, rows, width = out_ref.shape
    part = width - NOTE
    top = ids_ref.shape[1]
    lane = iota((rows, NOTE), 1)
    gates = gates_ref[...]
    first = gates.astype(BF).astype(F32)
    second = (gates - first).astype(BF).astype(F32)
    third = gates - first - second
    note = jnp.zeros((rows, NOTE), F32)
    for group, values in enumerate((ids_ref[...].astype(F32), first, second, third)):
        for k in range(top):
            note = jnp.where(lane == group * top + k, values[:, k : k + 1], note)
    for peer in range(peers):
        wanted = jnp.int32(0)
        for j in range(rows):
            slot = slot_ref[j]
            wanted += jnp.where(slot // column_span == peer, slot % rows, 0)
        own = jnp.where(lane == 4 * top, wanted.astype(F32), note)
        out_ref[peer, :, 0:part] = hidden_ref[:, peer * part : (peer + 1) * part]
        out_ref[peer, :, part:width] = own.astype(BF)


def route_kernel(top, arrived_ref, *refs):
    out_refs, weights_ref = refs[:-1], refs[-1]
    blocks, rows, width = arrived_ref.shape
    part = width - NOTE
    tokens = blocks * rows
    experts = out_refs[0].shape[0]
    stacked = jnp.concatenate([arrived_ref[b].astype(F32) for b in range(blocks)], axis=0)
    features = stacked[:, 0:part].astype(BF)
    note = stacked[:, part:width].T
    expert = iota((experts, tokens), 0).astype(F32)
    member = jnp.zeros((experts, tokens), F32)
    gate = jnp.zeros((experts, tokens), F32)
    for k in range(top):
        hit = note[k : k + 1, :] == expert
        value = note[top + k : top + k + 1, :] + note[2 * top + k : 2 * top + k + 1, :]
        value = value + note[3 * top + k : 3 * top + k + 1, :]
        member = jnp.where(hit, 1.0, member)
        gate = jnp.where(hit, value, gate)
    one, two = iota((tokens, tokens), 0), iota((tokens, tokens), 1)
    before = jnp.where((one // rows == two // rows) & (one < two), 1.0, 0.0).astype(BF)
    rank = dot(member.astype(BF), before)
    in_block = iota((blocks, tokens), 0) == iota((blocks, tokens), 1) // rows
    in_block = jnp.where(in_block, 1.0, 0.0)
    for c, out_ref in enumerate(out_refs):
        taken = jnp.where((member > 0.5) & (rank == float(c)), 1.0, 0.0)
        select = (taken[:, None, :] * in_block[None]).reshape(experts * blocks, tokens)
        weigh = ((taken * gate)[:, None, :] * in_block[None]).reshape(experts * blocks, tokens)
        out_ref[...] = dot(select.astype(BF), features).reshape(experts, blocks, part).astype(BF)
        high = weigh.astype(BF)
        weights_ref[c, 0] = high
        weights_ref[c, 1] = (weigh - high.astype(F32)).astype(BF)


def partial_kernel(place_ref, rows_ref, gate_ref, up_ref, send_ref, keep_ref):
    half = send_ref.shape[1]
    core = place_ref[1]
    keep_rows = rows_ref[pl.ds(pl.multiple_of(core * half, half), half), :]
    send_rows = rows_ref[pl.ds(pl.multiple_of((1 - core) * half, half), half), :]
    for which, weight_ref in enumerate((gate_ref, up_ref)):
        weight = weight_ref[...]
        send_ref[which] = dot(send_rows, weight).astype(BF)
        keep_ref[which] = dot(keep_rows, weight).astype(BF)


def pair_kernel(place_ref, keep_ref, got_ref, *out_refs):
    ring = len(out_refs)
    size = out_refs[0].shape[1]
    y = place_ref[0]
    for d, out_ref in enumerate(out_refs):
        start = pl.multiple_of(lax.rem(y + d, ring) * size, size)
        both = keep_ref[:, pl.ds(start, size), :].astype(F32)
        both += got_ref[:, pl.ds(start, size), :].astype(F32)
        out_ref[...] = both.astype(out_ref.dtype)


def units_kernel(own_ref, *refs):
    part_refs, out_ref = refs[:-1], refs[-1]
    total = own_ref[...]
    for part_ref in part_refs:
        total = total + part_ref[...].astype(F32)
    gate, up = total[0], total[1]
    out_ref[...] = (gate / (1.0 + jnp.exp(-gate)) * up).astype(BF)


def down_kernel(place_ref, *refs):
    ring = len(refs) - 3
    part_refs, other_ref, weight_ref, out_ref = refs[:ring], refs[-3], refs[-2], refs[-1]
    blocks = out_ref.shape[1]
    size = part_refs[0].shape[0]
    y, core = place_ref[0], place_ref[1]
    mine = jnp.concatenate([part_ref[...] for part_ref in part_refs], axis=0)
    for owner, rows in ((core, mine), (1 - core, other_ref[...])):
        result = dot(rows, weight_ref[...])
        for d in range(ring):
            start = owner * ring * (size // blocks) + lax.rem(y + d, ring) * (size // blocks)
            piece = result[d * size : (d + 1) * size].reshape(size // blocks, blocks, -1)
            out_ref[pl.ds(start, size // blocks)] = piece.astype(BF)


def combine_kernel(weights_ref, *refs):
    result_refs, out_ref = refs[:-1], refs[-1]
    total = 0.0
    for c, result_ref in enumerate(result_refs):
        experts, blocks, part = result_ref.shape
        results = result_ref[...].astype(F32).reshape(experts * blocks, part).astype(BF)
        for piece in range(2):
            total = total + dot(weights_ref[c, piece], results, ((0,), (0,)))
    out_ref[...] = total.reshape(out_ref.shape).astype(BF)


def spread_kernel(parts_ref, out_ref):
    peers, _, part = parts_ref.shape
    for peer in range(peers):
        out_ref[:, peer * part : (peer + 1) * part] = parts_ref[peer]


def stack_pairs(flat_ref, stacked_ref):
    rows = flat_ref.shape[0]
    total, span = stacked_ref.shape
    for p in range(0, total // rows, 2):
        both = [flat_ref[:, q * span : (q + 1) * span].astype(F32) for q in (p, p + 1)]
        stacked_ref[p * rows : (p + 2) * rows, :] = jnp.concatenate(both, axis=0).astype(BF)


def unstack_pairs(stacked, flat_ref):
    rows = flat_ref.shape[0]
    total, span = stacked.shape
    for p in range(total // rows):
        flat_ref[:, p * span : (p + 1) * span] = stacked[p * rows : (p + 1) * rows].astype(BF)


def pack_kernel(asked_ref, cache_ref, out_ref, stacked_ref):
    rows, pairs, span = out_ref.shape
    stack_pairs(cache_ref, stacked_ref)
    pair, column = iota((pairs, pairs * rows), 0), iota((pairs, pairs * rows), 1)
    same_pair = column // rows == pair
    select = [
        jnp.where(same_pair & (column % rows == asked_ref[r]), 1.0, 0.0) for r in range(rows)
    ]
    select = jnp.concatenate(select, axis=0).astype(BF)
    out_ref[...] = dot(select, stacked_ref[...]).reshape(rows, pairs, span).astype(BF)


def attend_kernel(
    source_ref, length_ref, arrived_ref, new_ref, queries_ref, cache_ref, mixed_ref,
    stacked_ref, keys_ref, out_ref,
):
    rows, pairs, span = arrived_ref.shape
    width = span // 2
    reach = -(-width // 128) * 128
    total = rows * pairs
    one, two = iota((total, total), 0), iota((total, total), 1)
    to_rows = (one // pairs == two % rows) & (one % pairs == two // rows)
    to_rows = jnp.where(to_rows, 1.0, 0.0).astype(BF)
    to_pairs = (one // rows == two % pairs) & (one % rows == two // pairs)
    to_pairs = jnp.where(to_pairs, 1.0, 0.0).astype(BF)
    stack_pairs(queries_ref, stacked_ref)
    queries = dot(to_rows, stacked_ref[...])
    turned = pltpu.roll(queries, width, 1)
    inside = iota((2 * pairs, reach), 1) < width
    pair, lane = iota((pairs, span), 0), iota((pairs, span), 1)
    column = iota((2 * pairs, 2 * pairs), 1)
    position = 2 * (column % pairs) + column // pairs
    for j in range(rows):
        length = length_ref[j]
        keys = arrived_ref[source_ref[j]].astype(F32)
        placed = (pair == length // 2) & ((lane >= width) == (length % 2 == 1))
        keys = jnp.where(placed, new_ref[j : j + 1, :], keys)
        keys_ref[j * pairs : (j + 1) * pairs, :] = keys.astype(BF)
        both = jnp.concatenate([keys, pltpu.roll(keys, width, 1)], axis=0)[:, 0:reach].astype(BF)
        own = slice(j * pairs, (j + 1) * pairs)
        heads = jnp.concatenate([queries[own, 0:reach], turned[own, 0:reach]], axis=0)
        heads = jnp.where(inside, heads, 0.0).astype(BF)
        scores = dot(heads, both, ((1,), (1,))) * score_scale
        scores = jnp.where(position <= length, scores, -jnp.inf)
        raised = jnp.exp(scores - jnp.max(scores, axis=1, keepdims=True))
        weights = (raised / jnp.sum(raised, axis=1, keepdims=True)).astype(BF)
        mixed = dot(weights, both[:, 0:LAT])
        mixed = jnp.concatenate([mixed[0:pairs], mixed[pairs:]], axis=1)
        out_ref[j * pairs : (j + 1) * pairs, :] = mixed.astype(BF)
    unstack_pairs(dot(to_pairs, keys_ref[...]), cache_ref)
    unstack_pairs(dot(to_pairs, out_ref[...]), mixed_ref)


def call(kernel, out_shape, in_specs, name, scratch=(), cost=None, **kw):
    return pl.pallas_call(
        kernel,
        out_shape=out_shape,
        in_specs=in_specs,
        out_specs=jax.tree.map(lambda _: VMEM, out_shape),
        scratch_shapes=list(scratch),
        compiler_params=PARAMS,
        cost_estimate=cost,
        name=name,
        **kw,
    )


def on_device(
    latent_cache,
    old_slot,
    lengths,
    new_latent,
    queries,
    hidden,
    expert_ids,
    expert_gates,
    gate_weight,
    up_weight,
    down_weight,
):
    rows, features = hidden.shape
    top = expert_ids.shape[1]
    peers = lax.axis_size("req")
    experts = lax.axis_size("exp")
    part = features // peers
    inner = gate_weight.shape[2]
    ring = peers // CORES
    me = lax.axis_index("req").astype(jnp.int32)
    place = jnp.stack([me // CORES, me % CORES])
    swap = [(k, k ^ 1) for k in range(peers)]

    def along(d):
        return [(k, (k + CORES * d) % peers) for k in range(peers)]

    column_span = experts * rows
    message = call(
        functools.partial(announce_kernel, column_span),
        shape_of((peers, rows, part + NOTE)),
        [SMEM, VMEM, VMEM, VMEM],
        "announce",
    )(old_slot, hidden, expert_ids, expert_gates)
    arrived = lax.all_to_all(message, "req", split_axis=0, concat_axis=0, tiled=True)

    *outgoing, weights = call(
        functools.partial(route_kernel, top),
        [shape_of((experts, peers, part))] * CAP + [shape_of((CAP, 2, experts * peers, peers * rows))],
        [VMEM],
        "route",
    )(arrived)

    width = new_latent.shape[1]
    span = 2 * width
    pairs = latent_cache.shape[1] // span
    asked = arrived[:, 0, part + 4 * top].astype(jnp.int32)
    packed = call(
        pack_kernel,
        shape_of((rows, pairs, span)),
        [SMEM, VMEM],
        "pack",
        [pltpu.VMEM((rows * pairs, span), BF)],
    )(asked, latent_cache)
    moved = lax.all_to_all(packed, "req", split_axis=0, concat_axis=0, tiled=True)

    slots = experts * peers
    half = slots // CORES
    size = half // ring
    gate_one, up_one, down_one = gate_weight[0], up_weight[0], down_weight[0]
    tile = min(inner, 512)
    returned = []
    for c in range(CAP):
        rows_here = lax.all_to_all(outgoing[c], "exp", split_axis=0, concat_axis=0, tiled=True)
        rows_here = rows_here.reshape(slots, part)
        send, keep = pl.pallas_call(
            partial_kernel,
            grid=(inner // tile,),
            out_shape=[shape_of((2, half, inner))] * 2,
            in_specs=[
                SMEM,
                pl.BlockSpec((slots, part), lambda i: (0, 0)),
                pl.BlockSpec((part, tile), lambda i: (0, i)),
                pl.BlockSpec((part, tile), lambda i: (0, i)),
            ],
            out_specs=[pl.BlockSpec((2, half, tile), lambda i: (0, 0, i))] * 2,
            compiler_params=PARAMS,
            name="partial",
        )(place, rows_here, gate_one, up_one)
        got = lax.ppermute(send, "req", swap)
        own, *sums = call(
            pair_kernel,
            [shape_of((2, size, inner), F32)] + [shape_of((2, size, inner))] * (ring - 1),
            [SMEM, VMEM, VMEM],
            "pair",
        )(place, keep, got)
        sums = [lax.ppermute(s, "req", along(d + 1)) for d, s in enumerate(sums)]
        units = call(
            units_kernel, shape_of((size, inner)), [VMEM] * ring, "units"
        )(own, *sums)
        gathered = [units] + [lax.ppermute(units, "req", along(-d)) for d in range(1, ring)]
        other = lax.ppermute(jnp.concatenate(gathered, axis=0), "req", swap)
        result = call(
            down_kernel,
            shape_of((experts, peers, part)),
            [SMEM] + [VMEM] * (ring + 2),
            "down",
        )(place, *gathered, other, down_one)
        returned.append(
            lax.all_to_all(result, "exp", split_axis=0, concat_axis=0, tiled=True)
        )

    combined = call(
        combine_kernel, shape_of((peers, rows, part)), [VMEM] * (CAP + 1), "combine"
    )(weights, *returned)
    parts = lax.all_to_all(combined, "req", split_axis=0, concat_axis=0, tiled=True)
    moe_out = call(spread_kernel, shape_of((rows, features)), [VMEM], "spread")(parts)

    new_pair = jnp.concatenate([new_latent, new_latent], axis=1).astype(F32)
    cache_out, attention = call(
        attend_kernel,
        [shape_of(latent_cache.shape), shape_of((rows, pairs * 2 * LAT))],
        [SMEM, SMEM, VMEM, VMEM, VMEM],
        "attend",
        [
            pltpu.VMEM((rows * pairs, span), BF),
            pltpu.VMEM((rows * pairs, span), BF),
            pltpu.VMEM((rows * pairs, 2 * LAT), BF),
        ],
    )(old_slot // column_span, lengths, moved, new_pair, queries)
    return (cache_out, attention, moe_out)


def solution(mesh):
    in_specs = (
        P(("req", "exp"), None),
        P(("req", "exp")),
        P(("req", "exp")),
        P(("req", "exp"), None),
        P(("req", "exp"), None),
        P(("req", "exp"), None),
        P(("req", "exp"), None),
        P(("req", "exp"), None),
        P("exp", "req", None),
        P("exp", "req", None),
        P("exp", None, "req"),
    )
    out_specs = (P(("req", "exp"), None), P(("req", "exp"), None), P(("req", "exp"), None))
    return jax.shard_map(
        on_device, mesh=mesh, in_specs=in_specs, out_specs=out_specs, check_vma=False
    )
```

profile of v0, /device:TPU:1, one launch (start us, length us, event | category | flops | bytes accessed | tf_op | source)
XLA Modules:
  0.0 213.1 jit_solution(14403597029874032003)
XLA Ops:
  0.7 1.0 copy-done.12
  1.7 0.7 copy-done.13
  2.4 0.7 copy-done.14
  3.7 0.8 announce.1
  4.5 11.0 %all_to_all.45.arrived_ref = bf16[8,8,1024]{2,1,0:T(8,128)(2,1)S(1)} all-to-all(bf16[8,8,1024]{2,1,0:T(8,128)(2,1)S(1)} %announce.1), channel_id=1, replica_groups=mesh['req'=8,'exp'=32] {'req'}, dimensions={0} | all-to-all | bytes 262144 | tf_op jit(solution)/shard_map/all_to_all | solution.py:271
  15.5 1.5 route.1
  17.0 0.8 copy-done.9
  17.8 0.7 copy-done.10
  18.5 25.2 %all_to_all.46 = bf16[32,8,896]{2,1,0:T(8,128)(2,1)S(1)} all-to-all(bf16[32,8,896]{2,1,0:T(8,128)(2,1)S(1)} %get-tuple-element.44), channel_id=1, replica_groups=mesh['req'=8,'exp'=32] {'exp'}, dimensions={0} | all-to-all | bytes 917504 | tf_op jit(solution)/shard_map/all_to_all | solution.py:300
  43.7 5.7 %all-to-all-start.4 = ((bf16[32,8,896]{2,1,0:T(8,128)(2,1)}), bf16[32,8,896]{2,1,0:T(8,128)(2,1)S(1)}, u32[]{:S(2)}, u32[]{:S(2)}) async-start(bf16[32,8,896]{2,1,0:T(8,128)(2,1)} %get-tuple-element.37), calls=%async_computation.4 | async-start | bytes 917504 | tf_op jit(solution)/shard_map/all_to_all | solution.py:300
  49.6 1.5 copy-done.1
  51.1 2.7 %partial.5 = (bf16[2,128,1024]{2,1,0:T(8,128)(2,1)}, bf16[2,128,1024]{2,1,0:T(8,128)(2,1)S(1)}) custom-call(s32[2]{0:T(128)S(1)} %pad_add_fusion.place_ref, bf16[256,896]{1,0:T(8,128)(2,1)S(1)} %bitcast.19, bf16[896,1024]{1,0:T(8,128)(2,1)S(1)} %bitcast.8, bf16[896,1024]{1,0:T(8,128)(2,1)S(1)} %bitcast.11), custom_call_target="tpu_custom_call" | custom-call | tf_op jit(solution)/shard_map/partial/pallas_call | solution.py:302
  53.8 1.8 collective-permute-start.16
  55.6 7.8 %all-to-all-done.4 = bf16[32,8,896]{2,1,0:T(8,128)(2,1)S(1)} async-done(((bf16[32,8,896]{2,1,0:T(8,128)(2,1)}), bf16[32,8,896]{2,1,0:T(8,128)(2,1)S(1)}, u32[]{:S(2)}, u32[]{:S(2)}) %all-to-all-start.4) | async-done | bytes 458784 | tf_op jit(solution)/shard_map/all_to_all | solution.py:300
  63.4 5.9 %all-to-all-start.2 = ((bf16[32,8,896]{2,1,0:T(8,128)(2,1)}), bf16[32,8,896]{2,1,0:T(8,128)(2,1)S(1)}, u32[]{:S(2)}, u32[]{:S(2)}) async-start(bf16[32,8,896]{2,1,0:T(8,128)(2,1)} %copy-done.9), calls=%async_computation.2 | async-start | bytes 917504 | tf_op jit(solution)/shard_map/all_to_all | solution.py:300
  69.4 1.3 pair.5
  71.0 1.8 collective-permute-start.18
  72.8 0.8 collective-permute-start.19
  73.6 4.0 %collective-permute-done.17.refs_0_ = bf16[2,32,1024]{2,1,0:T(8,128)(2,1)S(1)} collective-permute-done((bf16[2,32,1024]{2,1,0:T(8,128)(2,1)S(1)}, bf16[2,32,1024]{2,1,0:T(8,128)(2,1)S(1)}, u32[]{:S(2)}, u32[]{:S(2)}) %collective-permute-start.17) | collective-permute-done | bytes 131104 | tf_op jit(solution)/shard_map/ppermute | solution.py:323
  78.2 2.3 %collective-permute-start.20 = (bf16[32,1024]{1,0:T(8,128)(2,1)S(1)}, bf16[32,1024]{1,0:T(8,128)(2,1)S(1)}, u32[]{:S(2)}, u32[]{:S(2)}) collective-permute-start(bf16[32,1024]{1,0:T(8,128)(2,1)S(1)} %units.5.refs_0_), channel_id=1, source_target_pairs={{0,192},{32,224},{64,0},{96,32},{128,64},{160,96},{192,128},{224,1... | collective-permute-start | bytes 196616 | tf_op jit(solution)/shard_map/ppermute | solution.py:327
  80.5 0.7 collective-permute-start.22
  81.9 3.6 %collective-permute-done.21.refs_2_ = bf16[32,1024]{1,0:T(8,128)(2,1)S(1)} collective-permute-done((bf16[32,1024]{1,0:T(8,128)(2,1)S(1)}, bf16[32,1024]{1,0:T(8,128)(2,1)S(1)}, u32[]{:S(2)}, u32[]{:S(2)}) %collective-permute-start.21) | collective-permute-done | bytes 65568 | tf_op jit(solution)/shard_map/ppermute | solution.py:327
  85.9 4.6 %collective-permute-start.23 = (bf16[128,1024]{1,0:T(8,128)(2,1)S(1)}, bf16[128,1024]{1,0:T(8,128)(2,1)S(1)}, u32[]{:S(2)}, u32[]{:S(2)}) collective-permute-start(bf16[128,1024]{1,0:T(8,128)(2,1)S(1)} %pad_maximum_fusion.2), channel_id=1, source_target_pairs={{0,32},{32,0},{64,96},{96,64},{128,160},{160,128},{192,224},{224,1... | collective-permute-start | bytes 786440 | tf_op jit(solution)/shard_map/ppermute | solution.py:328
  90.5 2.7 %partial.4 = (bf16[2,128,1024]{2,1,0:T(8,128)(2,1)}, bf16[2,128,1024]{2,1,0:T(8,128)(2,1)S(1)}) custom-call(s32[2]{0:T(128)S(1)} %pad_add_fusion.place_ref, bf16[256,896]{1,0:T(8,128)(2,1)S(1)} %bitcast.18, bf16[896,1024]{1,0:T(8,128)(2,1)S(1)} %bitcast.9, bf16[896,1024]{1,0:T(8,128)(2,1)S(1)} %bitcast.12), custom_call_target="tpu_custom_call" | custom-call | tf_op jit(solution)/shard_map/partial/pallas_call | solution.py:302
  93.3 2.1 down.5
  95.3 9.7 %all-to-all-start.7 = ((bf16[32,8,896]{2,1,0:T(8,128)(2,1)}), bf16[32,8,896]{2,1,0:T(8,128)(2,1)S(1)}, u32[]{:S(2)}, u32[]{:S(2)}) async-start(bf16[32,8,896]{2,1,0:T(8,128)(2,1)} %down.5), calls=%async_computation.7 | async-start | bytes 917504 | tf_op jit(solution)/shard_map/all_to_all | solution.py:336
  105.1 1.3 pair.4
  106.4 1.1 collective-permute-start.10
  107.5 1.5 collective-permute-start.9
  109.0 3.3 %collective-permute-done.10.refs_1_ = bf16[2,32,1024]{2,1,0:T(8,128)(2,1)S(1)} collective-permute-done((bf16[2,32,1024]{2,1,0:T(8,128)(2,1)S(1)}, bf16[2,32,1024]{2,1,0:T(8,128)(2,1)S(1)}, u32[]{:S(2)}, u32[]{:S(2)}) %collective-permute-start.10) | collective-permute-done | bytes 131104 | tf_op jit(solution)/shard_map/ppermute | solution.py:323
  112.3 0.7 collective-permute-done.11.refs_2_
  113.0 2.8 %collective-permute-done.9.refs_0_ = bf16[2,32,1024]{2,1,0:T(8,128)(2,1)S(1)} collective-permute-done((bf16[2,32,1024]{2,1,0:T(8,128)(2,1)S(1)}, bf16[2,32,1024]{2,1,0:T(8,128)(2,1)S(1)}, u32[]{:S(2)}, u32[]{:S(2)}) %collective-permute-start.9) | collective-permute-done | bytes 131104 | tf_op jit(solution)/shard_map/ppermute | solution.py:323
  115.9 0.7 collective-permute-start.12
  116.6 0.8 collective-permute-start.13
  117.5 0.8 collective-permute-start.14
  118.2 1.2 collective-permute-done.12.refs_1_
  119.4 2.1 %collective-permute-done.13.refs_2_ = bf16[32,1024]{1,0:T(8,128)(2,1)S(1)} collective-permute-done((bf16[32,1024]{1,0:T(8,128)(2,1)S(1)}, bf16[32,1024]{1,0:T(8,128)(2,1)S(1)}, u32[]{:S(2)}, u32[]{:S(2)}) %collective-permute-start.13) | collective-permute-done | bytes 65568 | tf_op jit(solution)/shard_map/ppermute | solution.py:327
  121.5 0.9 collective-permute-done.14.refs_3_
  122.5 2.0 collective-permute-start.15
  124.5 2.7 %partial.3 = (bf16[2,128,1024]{2,1,0:T(8,128)(2,1)}, bf16[2,128,1024]{2,1,0:T(8,128)(2,1)S(1)}) custom-call(s32[2]{0:T(128)S(1)} %pad_add_fusion.place_ref, bf16[256,896]{1,0:T(8,128)(2,1)S(1)} %bitcast.17, bf16[896,1024]{1,0:T(8,128)(2,1)S(1)} %bitcast.10, bf16[896,1024]{1,0:T(8,128)(2,1)S(1)} %bitcast.13), custom_call_target="tpu_custom_call" | custom-call | tf_op jit(solution)/shard_map/partial/pallas_call | solution.py:302
  127.3 2.0 down.4
  129.3 9.5 %all-to-all-start.5 = ((bf16[32,8,896]{2,1,0:T(8,128)(2,1)}), bf16[32,8,896]{2,1,0:T(8,128)(2,1)S(1)}, u32[]{:S(2)}, u32[]{:S(2)}) async-start(bf16[32,8,896]{2,1,0:T(8,128)(2,1)} %down.4), calls=%async_computation.5 | async-start | bytes 917504 | tf_op jit(solution)/shard_map/all_to_all | solution.py:336
  138.8 1.2 pair.3
  140.1 2.2 %collective-permute-start.2 = (bf16[2,32,1024]{2,1,0:T(8,128)(2,1)S(1)}, bf16[2,32,1024]{2,1,0:T(8,128)(2,1)S(1)}, u32[]{:S(2)}, u32[]{:S(2)}) collective-permute-start(bf16[2,32,1024]{2,1,0:T(8,128)(2,1)S(1)} %get-tuple-element.35), channel_id=1, source_target_pairs={{0,128},{32,160},{64,192},{96,224},{128,0},{160,32},{192,64},{224,... | collective-permute-start | bytes 393224 | tf_op jit(solution)/shard_map/ppermute | solution.py:323
  142.7 3.3 %collective-permute-done.1.refs_0_ = bf16[2,32,1024]{2,1,0:T(8,128)(2,1)S(1)} collective-permute-done((bf16[2,32,1024]{2,1,0:T(8,128)(2,1)S(1)}, bf16[2,32,1024]{2,1,0:T(8,128)(2,1)S(1)}, u32[]{:S(2)}, u32[]{:S(2)}) %collective-permute-start.1) | collective-permute-done | bytes 131104 | tf_op jit(solution)/shard_map/ppermute | solution.py:323
  146.0 1.9 collective-permute-done.2.refs_1_
  147.9 0.8 collective-permute-done.3.refs_2_
  148.8 3.2 %collective-permute-start.4 = (bf16[32,1024]{1,0:T(8,128)(2,1)S(1)}, bf16[32,1024]{1,0:T(8,128)(2,1)S(1)}, u32[]{:S(2)}, u32[]{:S(2)}) collective-permute-start(bf16[32,1024]{1,0:T(8,128)(2,1)S(1)} %units.3.refs_0_), channel_id=1, source_target_pairs={{0,192},{32,224},{64,0},{96,32},{128,64},{160,96},{192,128},{224,1... | collective-permute-start | bytes 196616 | tf_op jit(solution)/shard_map/ppermute | solution.py:327
  152.0 0.7 collective-permute-start.6
  152.7 0.7 collective-permute-done.4.refs_1_
  153.3 3.4 %collective-permute-done.5.refs_2_ = bf16[32,1024]{1,0:T(8,128)(2,1)S(1)} collective-permute-done((bf16[32,1024]{1,0:T(8,128)(2,1)S(1)}, bf16[32,1024]{1,0:T(8,128)(2,1)S(1)}, u32[]{:S(2)}, u32[]{:S(2)}) %collective-permute-start.5) | collective-permute-done | bytes 65568 | tf_op jit(solution)/shard_map/ppermute | solution.py:327
  157.1 2.4 %collective-permute-start.7 = (bf16[128,1024]{1,0:T(8,128)(2,1)S(1)}, bf16[128,1024]{1,0:T(8,128)(2,1)S(1)}, u32[]{:S(2)}, u32[]{:S(2)}) collective-permute-start(bf16[128,1024]{1,0:T(8,128)(2,1)S(1)} %pad_maximum_fusion), channel_id=1, source_target_pairs={{0,32},{32,0},{64,96},{96,64},{128,160},{160,128},{192,224},{224,1... | collective-permute-start | bytes 786440 | tf_op jit(solution)/shard_map/ppermute | solution.py:328
  159.5 1.2 collective-permute-done.7.refs_4_
  160.6 2.0 down.3
  162.6 9.3 %all-to-all-start.3 = ((bf16[32,8,896]{2,1,0:T(8,128)(2,1)}), bf16[32,8,896]{2,1,0:T(8,128)(2,1)S(1)}, u32[]{:S(2)}, u32[]{:S(2)}) async-start(bf16[32,8,896]{2,1,0:T(8,128)(2,1)} %down.3), calls=%async_computation.3 | async-start | bytes 917504 | tf_op jit(solution)/shard_map/all_to_all | solution.py:336
  172.3 1.7 pack.1
  174.0 13.4 %all-to-all-done.3.refs_0_ = bf16[32,8,896]{2,1,0:T(8,128)(2,1)S(1)} async-done(((bf16[32,8,896]{2,1,0:T(8,128)(2,1)}), bf16[32,8,896]{2,1,0:T(8,128)(2,1)S(1)}, u32[]{:S(2)}, u32[]{:S(2)}) %all-to-all-start.3) | async-done | bytes 458784 | tf_op jit(solution)/shard_map/all_to_all | solution.py:336
  187.5 5.5 %all-to-all-start.1 = ((bf16[8,32,1152]{2,1,0:T(8,128)(2,1)}), bf16[8,32,1152]{2,1,0:T(8,128)(2,1)S(1)}, u32[]{:S(2)}, u32[]{:S(2)}) async-start(bf16[8,32,1152]{2,1,0:T(8,128)(2,1)} %pack.1), calls=%async_computation.1 | async-start | bytes 1179648 | tf_op jit(solution)/shard_map/all_to_all | solution.py:291
  193.0 1.0 copy-done.11
  194.0 1.2 combine.1
  195.3 7.9 %all-to-all-done.1.arrived_ref = bf16[8,32,1152]{2,1,0:T(8,128)(2,1)S(1)} async-done(((bf16[8,32,1152]{2,1,0:T(8,128)(2,1)}), bf16[8,32,1152]{2,1,0:T(8,128)(2,1)S(1)}, u32[]{:S(2)}, u32[]{:S(2)}) %all-to-all-start.1) | async-done | bytes 589856 | tf_op jit(solution)/shard_map/all_to_all | solution.py:291
  203.2 4.1 %all-to-all-start.8 = ((bf16[8,8,896]{2,1,0:T(8,128)(2,1)}), bf16[8,8,896]{2,1,0:T(8,128)(2,1)S(1)}, u32[]{:S(2)}, u32[]{:S(2)}) async-start(bf16[8,8,896]{2,1,0:T(8,128)(2,1)} %combine.1), calls=%async_computation.8 | async-start | bytes 229376 | tf_op jit(solution)/shard_map/all_to_all | solution.py:342
  207.3 5.1 %attend.1 = (bf16[8,36864]{1,0:T(8,128)(2,1)}, bf16[8,32768]{1,0:T(8,128)(2,1)}) custom-call(s32[8]{0:T(128)S(1)} %and_select_fusion.source_ref, s32[8]{0:T(128)S(1)} %copy-done.17, bf16[8,32,1152]{2,1,0:T(8,128)(2,1)S(1)} %all-to-all-done.1.arrived_ref, f32[8,1152]{1,0:T(8,128)S(1)} %maximum_convert_fusion.new_ref, bf16[8,36864]{1,0:T(8,128)(2,1)S(1)} %copy-done.8), custom_call_target="tpu_custom_call" | custom-call | tf_op jit(solution)/shard_map/attend/pallas_call | solution.py:346
  212.4 0.7 spread.1
  (63 shorter events, 4.4 us)
Async XLA Ops:
  0.6 48.9 %copy-start = (bf16[1,896,1024]{2,1,0:T(8,128)(2,1)S(1)}, bf16[1,896,1024]{2,1,0:T(8,128)(2,1)}, u32[]{:S(2)}) copy-start(bf16[1,896,1024]{2,1,0:T(8,128)(2,1)} %param.19) | copy-start | bytes 5505028
  0.6 1.0 copy-start.12
  1.7 0.7 copy-start.13
  2.4 0.7 copy-start.14
  3.0 0.7 copy-start.15
  17.0 0.8 copy-start.9
  17.8 0.7 copy-start.10
  43.7 19.7 %all-to-all-start.4 = ((bf16[32,8,896]{2,1,0:T(8,128)(2,1)}), bf16[32,8,896]{2,1,0:T(8,128)(2,1)S(1)}, u32[]{:S(2)}, u32[]{:S(2)}) async-start(bf16[32,8,896]{2,1,0:T(8,128)(2,1)} %get-tuple-element.37), calls=%async_computation.4 | async-start | bytes 917504 | tf_op jit(solution)/shard_map/all_to_all | solution.py:300
  49.6 1.5 copy-start.1
  53.8 15.6 %collective-permute-start.16 = (bf16[2,128,1024]{2,1,0:T(8,128)(2,1)}, bf16[2,128,1024]{2,1,0:T(8,128)(2,1)}, u32[]{:S(2)}, u32[]{:S(2)}) collective-permute-start(bf16[2,128,1024]{2,1,0:T(8,128)(2,1)} %get-tuple-element.46), channel_id=1, source_target_pairs={{0,32},{32,0},{64,96},{96,64},{128,160},{160,128},{192,224},{224,1... | collective-permute-start | bytes 1572872 | tf_op jit(solution)/shard_map/ppermute | solution.py:316
  63.4 31.9 %all-to-all-start.2 = ((bf16[32,8,896]{2,1,0:T(8,128)(2,1)}), bf16[32,8,896]{2,1,0:T(8,128)(2,1)S(1)}, u32[]{:S(2)}, u32[]{:S(2)}) async-start(bf16[32,8,896]{2,1,0:T(8,128)(2,1)} %copy-done.9), calls=%async_computation.2 | async-start | bytes 917504 | tf_op jit(solution)/shard_map/all_to_all | solution.py:300
  69.3 21.2 %copy-start.2 = (bf16[1,896,1024]{2,1,0:T(8,128)(2,1)S(1)}, bf16[1,896,1024]{2,1,0:T(8,128)(2,1)}, u32[]{:S(2)}) copy-start(bf16[1,896,1024]{2,1,0:T(8,128)(2,1)} %param.20) | copy-start | bytes 5505028
  70.7 7.0 %collective-permute-start.17 = (bf16[2,32,1024]{2,1,0:T(8,128)(2,1)S(1)}, bf16[2,32,1024]{2,1,0:T(8,128)(2,1)S(1)}, u32[]{:S(2)}, u32[]{:S(2)}) collective-permute-start(bf16[2,32,1024]{2,1,0:T(8,128)(2,1)S(1)} %get-tuple-element.48), channel_id=1, source_target_pairs={{0,64},{32,96},{64,128},{96,160},{128,192},{160,224},{192,0},{224,... | collective-permute-start | bytes 393224 | tf_op jit(solution)/shard_map/ppermute | solution.py:323
  71.0 6.6 %collective-permute-start.18 = (bf16[2,32,1024]{2,1,0:T(8,128)(2,1)S(1)}, bf16[2,32,1024]{2,1,0:T(8,128)(2,1)S(1)}, u32[]{:S(2)}, u32[]{:S(2)}) collective-permute-start(bf16[2,32,1024]{2,1,0:T(8,128)(2,1)S(1)} %get-tuple-element.49), channel_id=1, source_target_pairs={{0,128},{32,160},{64,192},{96,224},{128,0},{160,32},{192,64},{224,... | collective-permute-start | bytes 393224 | tf_op jit(solution)/shard_map/ppermute | solution.py:323
  72.8 5.3 %collective-permute-start.19 = (bf16[2,32,1024]{2,1,0:T(8,128)(2,1)S(1)}, bf16[2,32,1024]{2,1,0:T(8,128)(2,1)S(1)}, u32[]{:S(2)}, u32[]{:S(2)}) collective-permute-start(bf16[2,32,1024]{2,1,0:T(8,128)(2,1)S(1)} %get-tuple-element.50), channel_id=1, source_target_pairs={{0,192},{32,224},{64,0},{96,32},{128,64},{160,96},{192,128},{224,1... | collective-permute-start | bytes 393224 | tf_op jit(solution)/shard_map/ppermute | solution.py:323
  78.2 3.7 %collective-permute-start.20 = (bf16[32,1024]{1,0:T(8,128)(2,1)S(1)}, bf16[32,1024]{1,0:T(8,128)(2,1)S(1)}, u32[]{:S(2)}, u32[]{:S(2)}) collective-permute-start(bf16[32,1024]{1,0:T(8,128)(2,1)S(1)} %units.5.refs_0_), channel_id=1, source_target_pairs={{0,192},{32,224},{64,0},{96,32},{128,64},{160,96},{192,128},{224,1... | collective-permute-start | bytes 196616 | tf_op jit(solution)/shard_map/ppermute | solution.py:327
  80.5 4.9 %collective-permute-start.21 = (bf16[32,1024]{1,0:T(8,128)(2,1)S(1)}, bf16[32,1024]{1,0:T(8,128)(2,1)S(1)}, u32[]{:S(2)}, u32[]{:S(2)}) collective-permute-start(bf16[32,1024]{1,0:T(8,128)(2,1)S(1)} %units.5.refs_0_), channel_id=1, source_target_pairs={{0,128},{32,160},{64,192},{96,224},{128,0},{160,32},{192,64},{224,... | collective-permute-start | bytes 196616 | tf_op jit(solution)/shard_map/ppermute | solution.py:327
  80.5 5.3 %collective-permute-start.22 = (bf16[32,1024]{1,0:T(8,128)(2,1)S(1)}, bf16[32,1024]{1,0:T(8,128)(2,1)S(1)}, u32[]{:S(2)}, u32[]{:S(2)}) collective-permute-start(bf16[32,1024]{1,0:T(8,128)(2,1)S(1)} %units.5.refs_0_), channel_id=1, source_target_pairs={{0,64},{32,96},{64,128},{96,160},{128,192},{160,224},{192,0},{224,... | collective-permute-start | bytes 196616 | tf_op jit(solution)/shard_map/ppermute | solution.py:327
  85.9 7.4 %collective-permute-start.23 = (bf16[128,1024]{1,0:T(8,128)(2,1)S(1)}, bf16[128,1024]{1,0:T(8,128)(2,1)S(1)}, u32[]{:S(2)}, u32[]{:S(2)}) collective-permute-start(bf16[128,1024]{1,0:T(8,128)(2,1)S(1)} %pad_maximum_fusion.2), channel_id=1, source_target_pairs={{0,32},{32,0},{64,96},{96,64},{128,160},{160,128},{192,224},{224,1... | collective-permute-start | bytes 786440 | tf_op jit(solution)/shard_map/ppermute | solution.py:328
  90.5 2.8 %copy-start.4 = (bf16[1,1024,896]{2,1,0:T(8,128)(2,1)S(1)}, bf16[1,1024,896]{2,1,0:T(8,128)(2,1)}, u32[]{:S(2)}) copy-start(bf16[1,1024,896]{2,1,0:T(8,128)(2,1)} %param.21) | copy-start | bytes 5505028
  93.2 11.9 %collective-permute-start.8 = (bf16[2,128,1024]{2,1,0:T(8,128)(2,1)}, bf16[2,128,1024]{2,1,0:T(8,128)(2,1)}, u32[]{:S(2)}, u32[]{:S(2)}) collective-permute-start(bf16[2,128,1024]{2,1,0:T(8,128)(2,1)} %get-tuple-element.39), channel_id=1, source_target_pairs={{0,32},{32,0},{64,96},{96,64},{128,160},{160,128},{192,224},{224,1... | collective-permute-start | bytes 1572872 | tf_op jit(solution)/shard_map/ppermute | solution.py:316
  95.3 34.0 %all-to-all-start.7 = ((bf16[32,8,896]{2,1,0:T(8,128)(2,1)}), bf16[32,8,896]{2,1,0:T(8,128)(2,1)S(1)}, u32[]{:S(2)}, u32[]{:S(2)}) async-start(bf16[32,8,896]{2,1,0:T(8,128)(2,1)} %down.5), calls=%async_computation.7 | async-start | bytes 917504 | tf_op jit(solution)/shard_map/all_to_all | solution.py:336
  105.1 19.4 %copy-start.3 = (bf16[1,896,1024]{2,1,0:T(8,128)(2,1)S(1)}, bf16[1,896,1024]{2,1,0:T(8,128)(2,1)}, u32[]{:S(2)}) copy-start(bf16[1,896,1024]{2,1,0:T(8,128)(2,1)} %param.20) | copy-start | bytes 5505028
  106.4 5.9 %collective-permute-start.10 = (bf16[2,32,1024]{2,1,0:T(8,128)(2,1)S(1)}, bf16[2,32,1024]{2,1,0:T(8,128)(2,1)S(1)}, u32[]{:S(2)}, u32[]{:S(2)}) collective-permute-start(bf16[2,32,1024]{2,1,0:T(8,128)(2,1)S(1)} %get-tuple-element.42), channel_id=1, source_target_pairs={{0,128},{32,160},{64,192},{96,224},{128,0},{160,32},{192,64},{224,... | collective-permute-start | bytes 393224 | tf_op jit(solution)/shard_map/ppermute | solution.py:323
  107.5 5.5 %collective-permute-start.11 = (bf16[2,32,1024]{2,1,0:T(8,128)(2,1)S(1)}, bf16[2,32,1024]{2,1,0:T(8,128)(2,1)S(1)}, u32[]{:S(2)}, u32[]{:S(2)}) collective-permute-start(bf16[2,32,1024]{2,1,0:T(8,128)(2,1)S(1)} %get-tuple-element.43), channel_id=1, source_target_pairs={{0,192},{32,224},{64,0},{96,32},{128,64},{160,96},{192,128},{224,1... | collective-permute-start | bytes 393224 | tf_op jit(solution)/shard_map/ppermute | solution.py:323
  107.5 8.3 %collective-permute-start.9 = (bf16[2,32,1024]{2,1,0:T(8,128)(2,1)S(1)}, bf16[2,32,1024]{2,1,0:T(8,128)(2,1)S(1)}, u32[]{:S(2)}, u32[]{:S(2)}) collective-permute-start(bf16[2,32,1024]{2,1,0:T(8,128)(2,1)S(1)} %get-tuple-element.41), channel_id=1, source_target_pairs={{0,64},{32,96},{64,128},{96,160},{128,192},{160,224},{192,0},{224,... | collective-permute-start | bytes 393224 | tf_op jit(solution)/shard_map/ppermute | solution.py:323
  115.9 3.5 %collective-permute-start.12 = (bf16[32,1024]{1,0:T(8,128)(2,1)S(1)}, bf16[32,1024]{1,0:T(8,128)(2,1)S(1)}, u32[]{:S(2)}, u32[]{:S(2)}) collective-permute-start(bf16[32,1024]{1,0:T(8,128)(2,1)S(1)} %units.4.refs_0_), channel_id=1, source_target_pairs={{0,192},{32,224},{64,0},{96,32},{128,64},{160,96},{192,128},{224,1... | collective-permute-start | bytes 196616 | tf_op jit(solution)/shard_map/ppermute | solution.py:327
  116.6 4.9 %collective-permute-start.13 = (bf16[32,1024]{1,0:T(8,128)(2,1)S(1)}, bf16[32,1024]{1,0:T(8,128)(2,1)S(1)}, u32[]{:S(2)}, u32[]{:S(2)}) collective-permute-start(bf16[32,1024]{1,0:T(8,128)(2,1)S(1)} %units.4.refs_0_), channel_id=1, source_target_pairs={{0,128},{32,160},{64,192},{96,224},{128,0},{160,32},{192,64},{224,... | collective-permute-start | bytes 196616 | tf_op jit(solution)/shard_map/ppermute | solution.py:327
  117.5 5.0 %collective-permute-start.14 = (bf16[32,1024]{1,0:T(8,128)(2,1)S(1)}, bf16[32,1024]{1,0:T(8,128)(2,1)S(1)}, u32[]{:S(2)}, u32[]{:S(2)}) collective-permute-start(bf16[32,1024]{1,0:T(8,128)(2,1)S(1)} %units.4.refs_0_), channel_id=1, source_target_pairs={{0,64},{32,96},{64,128},{96,160},{128,192},{160,224},{192,0},{224,... | collective-permute-start | bytes 196616 | tf_op jit(solution)/shard_map/ppermute | solution.py:327
  122.5 4.8 %collective-permute-start.15 = (bf16[128,1024]{1,0:T(8,128)(2,1)S(1)}, bf16[128,1024]{1,0:T(8,128)(2,1)S(1)}, u32[]{:S(2)}, u32[]{:S(2)}) collective-permute-start(bf16[128,1024]{1,0:T(8,128)(2,1)S(1)} %pad_maximum_fusion.1), channel_id=1, source_target_pairs={{0,32},{32,0},{64,96},{96,64},{128,160},{160,128},{192,224},{224,1... | collective-permute-start | bytes 786440 | tf_op jit(solution)/shard_map/ppermute | solution.py:328
  124.5 2.8 %copy-start.5 = (bf16[1,1024,896]{2,1,0:T(8,128)(2,1)S(1)}, bf16[1,1024,896]{2,1,0:T(8,128)(2,1)}, u32[]{:S(2)}) copy-start(bf16[1,1024,896]{2,1,0:T(8,128)(2,1)} %param.21) | copy-start | bytes 5505028
  127.2 11.6 %collective-permute-start = (bf16[2,128,1024]{2,1,0:T(8,128)(2,1)}, bf16[2,128,1024]{2,1,0:T(8,128)(2,1)}, u32[]{:S(2)}, u32[]{:S(2)}) collective-permute-start(bf16[2,128,1024]{2,1,0:T(8,128)(2,1)} %get-tuple-element.32), channel_id=1, source_target_pairs={{0,32},{32,0},{64,96},{96,64},{128,160},{160,128},{192,224},{224,1... | collective-permute-start | bytes 1572872 | tf_op jit(solution)/shard_map/ppermute | solution.py:316
  129.3 31.3 %copy-start.6 = (bf16[1,1024,896]{2,1,0:T(8,128)(2,1)S(1)}, bf16[1,1024,896]{2,1,0:T(8,128)(2,1)}, u32[]{:S(2)}) copy-start(bf16[1,1024,896]{2,1,0:T(8,128)(2,1)} %param.21) | copy-start | bytes 5505028
  129.3 33.4 %all-to-all-start.5 = ((bf16[32,8,896]{2,1,0:T(8,128)(2,1)}), bf16[32,8,896]{2,1,0:T(8,128)(2,1)S(1)}, u32[]{:S(2)}, u32[]{:S(2)}) async-start(bf16[32,8,896]{2,1,0:T(8,128)(2,1)} %down.4), calls=%async_computation.5 | async-start | bytes 917504 | tf_op jit(solution)/shard_map/all_to_all | solution.py:336
  140.0 6.0 %collective-permute-start.1 = (bf16[2,32,1024]{2,1,0:T(8,128)(2,1)S(1)}, bf16[2,32,1024]{2,1,0:T(8,128)(2,1)S(1)}, u32[]{:S(2)}, u32[]{:S(2)}) collective-permute-start(bf16[2,32,1024]{2,1,0:T(8,128)(2,1)S(1)} %get-tuple-element.34), channel_id=1, source_target_pairs={{0,64},{32,96},{64,128},{96,160},{128,192},{160,224},{192,0},{224,... | collective-permute-start | bytes 393224 | tf_op jit(solution)/shard_map/ppermute | solution.py:323
  140.1 7.9 %collective-permute-start.2 = (bf16[2,32,1024]{2,1,0:T(8,128)(2,1)S(1)}, bf16[2,32,1024]{2,1,0:T(8,128)(2,1)S(1)}, u32[]{:S(2)}, u32[]{:S(2)}) collective-permute-start(bf16[2,32,1024]{2,1,0:T(8,128)(2,1)S(1)} %get-tuple-element.35), channel_id=1, source_target_pairs={{0,128},{32,160},{64,192},{96,224},{128,0},{160,32},{192,64},{224,... | collective-permute-start | bytes 393224 | tf_op jit(solution)/shard_map/ppermute | solution.py:323
  142.3 6.4 %collective-permute-start.3 = (bf16[2,32,1024]{2,1,0:T(8,128)(2,1)S(1)}, bf16[2,32,1024]{2,1,0:T(8,128)(2,1)S(1)}, u32[]{:S(2)}, u32[]{:S(2)}) collective-permute-start(bf16[2,32,1024]{2,1,0:T(8,128)(2,1)S(1)} %get-tuple-element.36), channel_id=1, source_target_pairs={{0,192},{32,224},{64,0},{96,32},{128,64},{160,96},{192,128},{224,1... | collective-permute-start | bytes 393224 | tf_op jit(solution)/shard_map/ppermute | solution.py:323
  148.8 4.5 %collective-permute-start.4 = (bf16[32,1024]{1,0:T(8,128)(2,1)S(1)}, bf16[32,1024]{1,0:T(8,128)(2,1)S(1)}, u32[]{:S(2)}, u32[]{:S(2)}) collective-permute-start(bf16[32,1024]{1,0:T(8,128)(2,1)S(1)} %units.3.refs_0_), channel_id=1, source_target_pairs={{0,192},{32,224},{64,0},{96,32},{128,64},{160,96},{192,128},{224,1... | collective-permute-start | bytes 196616 | tf_op jit(solution)/shard_map/ppermute | solution.py:327
  152.0 4.7 %collective-permute-start.5 = (bf16[32,1024]{1,0:T(8,128)(2,1)S(1)}, bf16[32,1024]{1,0:T(8,128)(2,1)S(1)}, u32[]{:S(2)}, u32[]{:S(2)}) collective-permute-start(bf16[32,1024]{1,0:T(8,128)(2,1)S(1)} %units.3.refs_0_), channel_id=1, source_target_pairs={{0,128},{32,160},{64,192},{96,224},{128,0},{160,32},{192,64},{224,... | collective-permute-start | bytes 196616 | tf_op jit(solution)/shard_map/ppermute | solution.py:327
  152.0 5.0 %collective-permute-start.6 = (bf16[32,1024]{1,0:T(8,128)(2,1)S(1)}, bf16[32,1024]{1,0:T(8,128)(2,1)S(1)}, u32[]{:S(2)}, u32[]{:S(2)}) collective-permute-start(bf16[32,1024]{1,0:T(8,128)(2,1)S(1)} %units.3.refs_0_), channel_id=1, source_target_pairs={{0,64},{32,96},{64,128},{96,160},{128,192},{160,224},{192,0},{224,... | collective-permute-start | bytes 196616 | tf_op jit(solution)/shard_map/ppermute | solution.py:327
  157.0 15.3 %copy-start.7 = (bf16[8,36864]{1,0:T(8,128)(2,1)S(1)}, bf16[8,36864]{1,0:T(8,128)(2,1)}, u32[]{:S(2)}) copy-start(bf16[8,36864]{1,0:T(8,128)(2,1)} %cache_ref.1) | copy-start | bytes 1769476
  157.1 3.6 %collective-permute-start.7 = (bf16[128,1024]{1,0:T(8,128)(2,1)S(1)}, bf16[128,1024]{1,0:T(8,128)(2,1)S(1)}, u32[]{:S(2)}, u32[]{:S(2)}) collective-permute-start(bf16[128,1024]{1,0:T(8,128)(2,1)S(1)} %pad_maximum_fusion), channel_id=1, source_target_pairs={{0,32},{32,0},{64,96},{96,64},{128,160},{160,128},{192,224},{224,1... | collective-permute-start | bytes 786440 | tf_op jit(solution)/shard_map/ppermute | solution.py:328
  162.6 30.3 %copy-start.18 = (bf16[8,576]{1,0:T(8,128)(2,1)S(1)}, bf16[8,576]{1,0:T(8,128)(2,1)}, u32[]{:S(2)}) copy-start(bf16[8,576]{1,0:T(8,128)(2,1)} %param.14) | copy-start | bytes 27652
  162.6 24.8 %all-to-all-start.3 = ((bf16[32,8,896]{2,1,0:T(8,128)(2,1)}), bf16[32,8,896]{2,1,0:T(8,128)(2,1)S(1)}, u32[]{:S(2)}, u32[]{:S(2)}) async-start(bf16[32,8,896]{2,1,0:T(8,128)(2,1)} %down.3), calls=%async_computation.3 | async-start | bytes 917504 | tf_op jit(solution)/shard_map/all_to_all | solution.py:336
  174.0 33.3 %copy-start.16 = (s32[8]{0:T(128)S(1)}, s32[8]{0:T(128)}, u32[]{:S(2)}) copy-start(s32[8]{0:T(128)} %slot_ref.1) | copy-start | bytes 100
  174.0 33.3 %copy-start.8 = (bf16[8,36864]{1,0:T(8,128)(2,1)S(1)}, bf16[8,36864]{1,0:T(8,128)(2,1)}, u32[]{:S(2)}) copy-start(bf16[8,36864]{1,0:T(8,128)(2,1)} %queries_ref.1) | copy-start | bytes 1769476
  174.0 33.3 %copy-start.17 = (s32[8]{0:T(128)S(1)}, s32[8]{0:T(128)}, u32[]{:S(2)}) copy-start(s32[8]{0:T(128)} %length_ref.1) | copy-start | bytes 100
  187.5 15.7 %all-to-all-start.1 = ((bf16[8,32,1152]{2,1,0:T(8,128)(2,1)}), bf16[8,32,1152]{2,1,0:T(8,128)(2,1)S(1)}, u32[]{:S(2)}, u32[]{:S(2)}) async-start(bf16[8,32,1152]{2,1,0:T(8,128)(2,1)} %pack.1), calls=%async_computation.1 | async-start | bytes 1179648 | tf_op jit(solution)/shard_map/all_to_all | solution.py:291
  193.0 1.0 copy-start.11
  203.2 9.3 %all-to-all-start.8 = ((bf16[8,8,896]{2,1,0:T(8,128)(2,1)}), bf16[8,8,896]{2,1,0:T(8,128)(2,1)S(1)}, u32[]{:S(2)}, u32[]{:S(2)}) async-start(bf16[8,8,896]{2,1,0:T(8,128)(2,1)} %combine.1), calls=%async_computation.8 | async-start | bytes 229376 | tf_op jit(solution)/shard_map/all_to_all | solution.py:342
where the time goes:
time: 214 us; the launch traced here: 213 us
  starting transfers between devices  78.2 us (37%)
  waiting for transfers between devices  60.9 us (28%)
  blocking collectives  36.3 us (17%)
  Pallas kernels  29.2 us (14%)
  local copies, waits for them, and re-layouts  7.13 us (3%)
    all_to_all x3, starting transfers between devices, on_device(): lax.all_to_all(result, 'exp', split_axis=0, concat_axis=0, tiled=True)  28.6 us
    all_to_all x1, blocking collectives, on_device(): lax.all_to_all(outgoing[c], 'exp', split_axis=0, concat_axis=0, tiled=True)  25.2 us
    ppermute x9, waiting for transfers between devices, on_device(): sums = [lax.ppermute(s, 'req', along(d + 1)) for d, s in enumerate(sums)]  17.3 us
    all_to_all x3, waiting for transfers between devices, on_device(): lax.all_to_all(result, 'exp', split_axis=0, concat_axis=0, tiled=True)  13.4 us
    ppermute x9, waiting for transfers between devices, on_device(): lax.ppermute(units, 'req', along(-d))  13.3 us
    all_to_all x2, starting transfers between devices, on_device(): lax.all_to_all(outgoing[c], 'exp', split_axis=0, concat_axis=0, tiled=True)  11.7 us
    all_to_all x1, blocking collectives, on_device(): lax.all_to_all(message, 'req', split_axis=0, concat_axis=0, tiled=True)  11 us
    ppermute x9, starting transfers between devices, on_device(): lax.ppermute(units, 'req', along(-d))  9.18 us
  transfers between devices with their start and end apart: 31, of which 21 were waited for; matrix products, arithmetic and copies ran while one was open for 0% of the time, Pallas kernels for 12%

commit v1 on v0

--- a/solution.py
+++ b/solution.py
@@ -11,6 +11,8 @@
 CAP = 3
 CORES = 2
 NOTE = 128
+SEND = ((0, 1, 2),)
+WORK = ((0, 1, 2),)
 
 score_scale = 0.07216878364870323
 
@@ -56,8 +58,8 @@
         out_ref[peer, :, part:width] = own.astype(BF)
 
 
-def route_kernel(top, arrived_ref, *refs):
-    out_refs, weights_ref = refs[:-1], refs[-1]
+def route_kernel(top, groups, arrived_ref, *refs):
+    out_refs, weights_refs = refs[: len(groups[0])], refs[len(groups[0]) :]
     blocks, rows, width = arrived_ref.shape
     part = width - NOTE
     tokens = blocks * rows
@@ -79,25 +81,34 @@
     rank = dot(member.astype(BF), before)
     in_block = iota((blocks, tokens), 0) == iota((blocks, tokens), 1) // rows
     in_block = jnp.where(in_block, 1.0, 0.0)
-    for c, out_ref in enumerate(out_refs):
-        taken = jnp.where((member > 0.5) & (rank == float(c)), 1.0, 0.0)
-        select = (taken[:, None, :] * in_block[None]).reshape(experts * blocks, tokens)
-        weigh = ((taken * gate)[:, None, :] * in_block[None]).reshape(experts * blocks, tokens)
-        out_ref[...] = dot(select.astype(BF), features).reshape(experts, blocks, part).astype(BF)
+    taken = [jnp.where((member > 0.5) & (rank == float(c)), 1.0, 0.0) for c in range(CAP)]
+
+    def slots_of(ranks, factor):
+        pieces = [(taken[c] * factor)[:, None, :] * in_block[None] for c in ranks]
+        both = jnp.concatenate(pieces, axis=1) if len(pieces) > 1 else pieces[0]
+        return both.reshape(experts * len(ranks) * blocks, tokens)
+
+    for ranks, out_ref in zip(groups[0], out_refs):
+        select = slots_of(ranks, 1.0).astype(BF)
+        out_ref[...] = dot(select, features).reshape(out_ref.shape).astype(BF)
+    for ranks, weights_ref in zip(groups[1], weights_refs):
+        weigh = slots_of(ranks, gate)
         high = weigh.astype(BF)
-        weights_ref[c, 0] = high
-        weights_ref[c, 1] = (weigh - high.astype(F32)).astype(BF)
-
-
-def partial_kernel(place_ref, rows_ref, gate_ref, up_ref, send_ref, keep_ref):
-    half = send_ref.shape[1]
+        weights_ref[0] = high
+        weights_ref[1] = (weigh - high.astype(F32)).astype(BF)
+
+
+def partial_kernel(other_core, low, place_ref, rows_ref, gate_ref, up_ref, *refs):
+    out_ref = refs[-1]
+    half = rows_ref.shape[0] // CORES
+    part = rows_ref.shape[2]
+    each = out_ref.shape[1] // half
     core = place_ref[1]
-    keep_rows = rows_ref[pl.ds(pl.multiple_of(core * half, half), half), :]
-    send_rows = rows_ref[pl.ds(pl.multiple_of((1 - core) * half, half), half), :]
-    for which, weight_ref in enumerate((gate_ref, up_ref)):
-        weight = weight_ref[...]
-        send_ref[which] = dot(send_rows, weight).astype(BF)
-        keep_ref[which] = dot(keep_rows, weight).astype(BF)
+    core = 1 - core if other_core else core
+    rows = rows_ref[pl.ds(core * half, half)].astype(F32)
+    rows = rows[:, low : low + each, :].reshape(half * each, part).astype(BF)
+    out_ref[0] = dot(rows, gate_ref[...]).astype(BF)
+    out_ref[1] = dot(rows, up_ref[...]).astype(BF)
 
 
 def pair_kernel(place_ref, keep_ref, got_ref, *out_refs):
@@ -123,26 +134,28 @@
 def down_kernel(place_ref, *refs):
     ring = len(refs) - 3
     part_refs, other_ref, weight_ref, out_ref = refs[:ring], refs[-3], refs[-2], refs[-1]
-    blocks = out_ref.shape[1]
+    each = out_ref.shape[1]
     size = part_refs[0].shape[0]
+    count = size // each
     y, core = place_ref[0], place_ref[1]
     mine = jnp.concatenate([part_ref[...] for part_ref in part_refs], axis=0)
     for owner, rows in ((core, mine), (1 - core, other_ref[...])):
         result = dot(rows, weight_ref[...])
         for d in range(ring):
-            start = owner * ring * (size // blocks) + lax.rem(y + d, ring) * (size // blocks)
-            piece = result[d * size : (d + 1) * size].reshape(size // blocks, blocks, -1)
-            out_ref[pl.ds(start, size // blocks)] = piece.astype(BF)
-
-
-def combine_kernel(weights_ref, *refs):
-    result_refs, out_ref = refs[:-1], refs[-1]
+            start = owner * ring * count + lax.rem(y + d, ring) * count
+            piece = result[d * size : (d + 1) * size].reshape(count, each, -1)
+            out_ref[pl.ds(start, count)] = piece.astype(BF)
+
+
+def combine_kernel(*refs):
+    count = len(refs) // 2
+    weights_refs, result_refs, out_ref = refs[:count], refs[count:-1], refs[-1]
     total = 0.0
-    for c, result_ref in enumerate(result_refs):
-        experts, blocks, part = result_ref.shape
-        results = result_ref[...].astype(F32).reshape(experts * blocks, part).astype(BF)
+    for weights_ref, result_ref in zip(weights_refs, result_refs):
+        experts, each, part = result_ref.shape
+        results = result_ref[...].astype(F32).reshape(experts * each, part).astype(BF)
         for piece in range(2):
-            total = total + dot(weights_ref[c, piece], results, ((0,), (0,)))
+            total = total + dot(weights_ref[piece], results, ((0,), (0,)))
     out_ref[...] = total.reshape(out_ref.shape).astype(BF)
 
 
@@ -167,8 +180,10 @@
         flat_ref[:, p * span : (p + 1) * span] = stacked[p * rows : (p + 1) * rows].astype(BF)
 
 
-def pack_kernel(asked_ref, cache_ref, out_ref, stacked_ref):
-    rows, pairs, span = out_ref.shape
+def pack_kernel(asked_ref, cache_ref, *refs):
+    out_refs, stacked_ref = refs[:-1], refs[-1]
+    rows = len(out_refs)
+    pairs, span = out_refs[0].shape
     stack_pairs(cache_ref, stacked_ref)
     pair, column = iota((pairs, pairs * rows), 0), iota((pairs, pairs * rows), 1)
     same_pair = column // rows == pair
@@ -176,14 +191,18 @@
         jnp.where(same_pair & (column % rows == asked_ref[r]), 1.0, 0.0) for r in range(rows)
     ]
     select = jnp.concatenate(select, axis=0).astype(BF)
-    out_ref[...] = dot(select, stacked_ref[...]).reshape(rows, pairs, span).astype(BF)
+    packed = dot(select, stacked_ref[...])
+    for r, out_ref in enumerate(out_refs):
+        out_ref[...] = packed[r * pairs : (r + 1) * pairs].astype(BF)
 
 
 def attend_kernel(
-    source_ref, length_ref, arrived_ref, new_ref, queries_ref, cache_ref, mixed_ref,
-    stacked_ref, keys_ref, out_ref,
+    source_ref, length_ref, new_ref, queries_ref, *refs
 ):
+    cache_ref, mixed_ref, arrived_ref, stacked_ref, keys_ref, out_ref = refs[-6:]
     rows, pairs, span = arrived_ref.shape
+    for d, moved_ref in enumerate(refs[:-6]):
+        arrived_ref[d] = moved_ref[...].astype(F32)
     width = span // 2
     reach = -(-width // 128) * 128
     total = rows * pairs
@@ -201,7 +220,7 @@
     position = 2 * (column % pairs) + column // pairs
     for j in range(rows):
         length = length_ref[j]
-        keys = arrived_ref[source_ref[j]].astype(F32)
+        keys = arrived_ref[source_ref[j]]
         placed = (pair == length // 2) & ((lane >= width) == (length % 2 == 1))
         keys = jnp.where(placed, new_ref[j : j + 1, :], keys)
         keys_ref[j * pairs : (j + 1) * pairs, :] = keys.astype(BF)
@@ -270,50 +289,80 @@
     )(old_slot, hidden, expert_ids, expert_gates)
     arrived = lax.all_to_all(message, "req", split_axis=0, concat_axis=0, tiled=True)
 
-    *outgoing, weights = call(
-        functools.partial(route_kernel, top),
-        [shape_of((experts, peers, part))] * CAP + [shape_of((CAP, 2, experts * peers, peers * rows))],
+    routed = call(
+        functools.partial(route_kernel, top, (SEND, WORK)),
+        [shape_of((experts, peers * len(g), part)) for g in SEND]
+        + [shape_of((2, experts * peers * len(g), peers * rows)) for g in WORK],
         [VMEM],
         "route",
     )(arrived)
+    outgoing, weights = routed[: len(SEND)], routed[len(SEND) :]
 
     width = new_latent.shape[1]
     span = 2 * width
     pairs = latent_cache.shape[1] // span
     asked = arrived[:, 0, part + 4 * top].astype(jnp.int32)
+    asked = jnp.roll(asked, -me)
     packed = call(
         pack_kernel,
-        shape_of((rows, pairs, span)),
+        [shape_of((pairs, span))] * peers,
         [SMEM, VMEM],
         "pack",
         [pltpu.VMEM((rows * pairs, span), BF)],
     )(asked, latent_cache)
-    moved = lax.all_to_all(packed, "req", split_axis=0, concat_axis=0, tiled=True)
-
-    slots = experts * peers
-    half = slots // CORES
-    size = half // ring
+    moved = [packed[0]] + [
+        lax.ppermute(packed[d], "req", [(k, (k + d) % peers) for k in range(peers)])
+        for d in range(1, peers)
+    ]
+    new_pair = jnp.concatenate([new_latent, new_latent], axis=1).astype(F32)
+    source = lax.rem(me - old_slot // column_span + peers, peers)
+    cache_out, attention = call(
+        attend_kernel,
+        [shape_of(latent_cache.shape), shape_of((rows, pairs * 2 * LAT))],
+        [SMEM, SMEM, VMEM, VMEM] + [VMEM] * peers,
+        "attend",
+        [
+            pltpu.VMEM((rows, pairs, span), F32),
+            pltpu.VMEM((rows * pairs, span), BF),
+            pltpu.VMEM((rows * pairs, span), BF),
+            pltpu.VMEM((rows * pairs, 2 * LAT), BF),
+        ],
+    )(source, lengths, new_pair, queries, *moved)
+
     gate_one, up_one, down_one = gate_weight[0], up_weight[0], down_weight[0]
     tile = min(inner, 512)
-    returned = []
-    for c in range(CAP):
-        rows_here = lax.all_to_all(outgoing[c], "exp", split_axis=0, concat_axis=0, tiled=True)
-        rows_here = rows_here.reshape(slots, part)
-        send, keep = pl.pallas_call(
-            partial_kernel,
+    received = [
+        lax.all_to_all(o, "exp", split_axis=0, concat_axis=0, tiled=True) for o in outgoing
+    ]
+    where_of = {c: (i, g.index(c) * peers) for i, g in enumerate(SEND) for c in g}
+
+    def partial(other_core, group, after):
+        i, low = where_of[group[0]]
+        each = peers * len(group)
+        half = experts // CORES * each
+        return pl.pallas_call(
+            functools.partial(partial_kernel, other_core, low),
             grid=(inner // tile,),
-            out_shape=[shape_of((2, half, inner))] * 2,
+            out_shape=shape_of((2, half, inner)),
             in_specs=[
                 SMEM,
-                pl.BlockSpec((slots, part), lambda i: (0, 0)),
+                pl.BlockSpec(received[i].shape, lambda i: (0, 0, 0)),
                 pl.BlockSpec((part, tile), lambda i: (0, i)),
                 pl.BlockSpec((part, tile), lambda i: (0, i)),
-            ],
-            out_specs=[pl.BlockSpec((2, half, tile), lambda i: (0, 0, i))] * 2,
+            ]
+            + [pl.BlockSpec(memory_space=pl.ANY)] * len(after),
+            out_specs=pl.BlockSpec((2, half, tile), lambda i: (0, 0, i)),
             compiler_params=PARAMS,
             name="partial",
-        )(place, rows_here, gate_one, up_one)
+        )(place, received[i], gate_one, up_one, *after)
+
+    returned = []
+    for group in WORK:
+        each = peers * len(group)
+        size = experts // CORES * each // ring
+        send = partial(True, group, [cache_out])
         got = lax.ppermute(send, "req", swap)
+        keep = partial(False, group, [send])
         own, *sums = call(
             pair_kernel,
             [shape_of((2, size, inner), F32)] + [shape_of((2, size, inner))] * (ring - 1),
@@ -321,39 +370,22 @@
             "pair",
         )(place, keep, got)
         sums = [lax.ppermute(s, "req", along(d + 1)) for d, s in enumerate(sums)]
-        units = call(
-            units_kernel, shape_of((size, inner)), [VMEM] * ring, "units"
-        )(own, *sums)
+        units = call(units_kernel, shape_of((size, inner)), [VMEM] * ring, "units")(own, *sums)
         gathered = [units] + [lax.ppermute(units, "req", along(-d)) for d in range(1, ring)]
         other = lax.ppermute(jnp.concatenate(gathered, axis=0), "req", swap)
         result = call(
             down_kernel,
-            shape_of((experts, peers, part)),
+            shape_of((experts, each, part)),
             [SMEM] + [VMEM] * (ring + 2),
             "down",
         )(place, *gathered, other, down_one)
-        returned.append(
-            lax.all_to_all(result, "exp", split_axis=0, concat_axis=0, tiled=True)
-        )
+        returned.append(lax.all_to_all(result, "exp", split_axis=0, concat_axis=0, tiled=True))
 
     combined = call(
-        combine_kernel, shape_of((peers, rows, part)), [VMEM] * (CAP + 1), "combine"
-    )(weights, *returned)
+        combine_kernel, shape_of((peers, rows, part)), [VMEM] * (2 * len(WORK)), "combine"
+    )(*weights, *returned)
     parts = lax.all_to_all(combined, "req", split_axis=0, concat_axis=0, tiled=True)
     moe_out = call(spread_kernel, shape_of((rows, features)), [VMEM], "spread")(parts)
-
-    new_pair = jnp.concatenate([new_latent, new_latent], axis=1).astype(F32)
-    cache_out, attention = call(
-        attend_kernel,
-        [shape_of(latent_cache.shape), shape_of((rows, pairs * 2 * LAT))],
-        [SMEM, SMEM, VMEM, VMEM, VMEM],
-        "attend",
-        [
-            pltpu.VMEM((rows * pairs, span), BF),
-            pltpu.VMEM((rows * pairs, span), BF),
-            pltpu.VMEM((rows * pairs, 2 * LAT), BF),
-        ],
-    )(old_slot // column_span, lengths, moved, new_pair, queries)
     return (cache_out, attention, moe_out)
 
 

time: 214 us -> 167 us (0.78)
  starting transfers between devices: 78.2 us -> 30.9 us
  blocking collectives: 36.3 us -> 62.4 us
  waiting for transfers between devices: 60.9 us -> 41.3 us
  Pallas kernels: 29.2 us -> 19.6 us
  local copies, waits for them, and re-layouts: 7.13 us -> 11.3 us
    all_to_all x7 -> x1, starting transfers between devices: 49.8 us -> 11.2 us  [on_device(): lax.all_to_all(o, 'exp', split_axis=0, concat_axis=0, tiled=True)]
    all_to_all x1 -> x2, blocking collectives: 25.2 us -> 51.4 us  [the longest x1 40.8 us: on_device(): lax.all_to_all(result, 'exp', split_axis=0, concat_axis=0, tiled=True)]
    all_to_all x7 -> x1, waiting for transfers between devices: 29.2 us -> 7.93 us  [on_device(): lax.all_to_all(o, 'exp', split_axis=0, concat_axis=0, tiled=True)]
    ppermute x0 -> x7, starting transfers between devices: none -> 7.6 us  [on_device(): lax.ppermute(packed[d], 'req', [(k, (k + d) % peers) for k in range(peers)])]
    ppermute x3 -> x1, starting transfers between devices: 9 us -> 1.58 us  [on_device(): other = lax.ppermute(jnp.concatenate(gathered, axis=0), 'req', swap)]
    pallas_call x9 -> x6, Pallas kernels: 18.7 us -> 11.8 us  [the longest x2 5.5 us: partial(): pl.pallas_call(functools.partial(partial_kernel, other_core, low), grid=(...]
    ppermute x9 -> x3, starting transfers between devices: 8.28 us -> 2.92 us  [on_device(): sums = [lax.ppermute(s, 'req', along(d + 1)) for d, s in enumerate(sums)]]
    ppermute x0 -> x7, waiting for transfers between devices: none -> 5.15 us  [on_device(): lax.ppermute(packed[d], 'req', [(k, (k + d) % peers) for k in range(peers)])]
  transfers between devices with their start and end apart: 31 -> 16, of which waited for: 21 -> 12; matrix products, arithmetic and copies ran while one was open for 0% -> 0% of each run, Pallas kernels for 12% -> 6%
where the time goes in v1:
time: 167 us
  blocking collectives  62.4 us (37%)
  waiting for transfers between devices  41.3 us (25%)
  starting transfers between devices  30.9 us (19%)
  Pallas kernels  19.6 us (12%)
  local copies, waits for them, and re-layouts  11.3 us (7%)
    all_to_all x1, blocking collectives, on_device(): lax.all_to_all(result, 'exp', split_axis=0, concat_axis=0, tiled=True)  40.8 us
    ppermute x3, waiting for transfers between devices, on_device(): sums = [lax.ppermute(s, 'req', along(d + 1)) for d, s in enumerate(sums)]  17.5 us
    all_to_all x1, starting transfers between devices, on_device(): lax.all_to_all(o, 'exp', split_axis=0, concat_axis=0, tiled=True)  11.2 us
    all_to_all x1, blocking collectives, on_device(): lax.all_to_all(message, 'req', split_axis=0, concat_axis=0, tiled=True)  11 us
    unnamed x38, local copies, waits for them, and re-layouts  11 us
    all_to_all x1, blocking collectives, on_device(): lax.all_to_all(combined, 'req', split_axis=0, concat_axis=0, tiled=True)  10.6 us
    ppermute x3, waiting for transfers between devices, on_device(): lax.ppermute(units, 'req', along(-d))  8.57 us
    all_to_all x1, waiting for transfers between devices, on_device(): lax.all_to_all(o, 'exp', split_axis=0, concat_axis=0, tiled=True)  7.93 us
  transfers between devices with their start and end apart: 16, of which 12 were waited for; matrix products, arithmetic and copies ran while one was open for 0% of the time, Pallas kernels for 6%

profile of v1, /device:TPU:1, one launch (start us, length us, event | category | flops | bytes accessed | tf_op | source)
XLA Modules:
  0.0 166.6 jit_solution(3932212635724597104)
XLA Ops:
  0.6 0.9 copy-done.8
  1.5 0.7 copy-done.9
  2.2 0.7 copy-done.10
  2.9 0.7 copy-done.11
  3.6 0.8 announce.1
  4.3 0.0 copy-start.18
  4.3 11.0 %all_to_all.20.arrived_ref = bf16[8,8,1024]{2,1,0:T(8,128)(2,1)S(1)} all-to-all(bf16[8,8,1024]{2,1,0:T(8,128)(2,1)S(1)} %announce.1), channel_id=1, replica_groups=mesh['req'=8,'exp'=32] {'req'}, dimensions={0} | all-to-all | bytes 262144 | tf_op jit(solution)/shard_map/all_to_all | solution.py:290
  15.4 1.9 %route.1 = (bf16[32,24,896]{2,1,0:T(8,128)(2,1)}, bf16[2,768,64]{2,1,0:T(8,128)(2,1)S(1)}) custom-call(bf16[8,8,1024]{2,1,0:T(8,128)(2,1)S(1)} %all_to_all.20.arrived_ref), custom_call_target="tpu_custom_call" | custom-call | tf_op jit(solution)/shard_map/route/pallas_call | solution.py:292
  17.3 0.8 copy-done.6
  18.1 11.2 %all-to-all-start.1 = ((bf16[32,24,896]{2,1,0:T(8,128)(2,1)}), bf16[32,24,896]{2,1,0:T(8,128)(2,1)S(1)}, u32[]{:S(2)}, u32[]{:S(2)}) async-start(bf16[32,24,896]{2,1,0:T(8,128)(2,1)} %get-tuple-element.30), calls=%async_computation.1 | async-start | bytes 2752512 | tf_op jit(solution)/shard_map/all_to_all | solution.py:335
  29.3 0.0 copy-start
  29.3 0.1 maximum_convert_fusion.new_ref
  29.4 0.2 slice_reduce_fusion
  29.6 0.1 maximum_convert_fusion.1
  29.7 0.1 dynamic_slice.4.asked_ref
  29.8 1.1 copy-done.4
  30.9 1.5 pack.1
  32.4 0.6 copy-done.14
  33.0 0.6 copy-done.15
  33.6 0.6 copy-done.16
  34.3 0.6 copy-done.17
  34.9 1.3 collective-permute-start
  36.2 0.0 collective-permute-start.1
  36.3 2.2 %collective-permute-start.2 = (bf16[32,1152]{1,0:T(8,128)(2,1)}, bf16[32,1152]{1,0:T(8,128)(2,1)S(1)}, u32[]{:S(2)}, u32[]{:S(2)}) collective-permute-start(bf16[32,1152]{1,0:T(8,128)(2,1)} %copy-done.17), channel_id=1, source_target_pairs={{0,96},{32,128},{64,160},{96,192},{128,224},{160,0},{192,32},{224,... | collective-permute-start | bytes 221192 | tf_op jit(solution)/shard_map/ppermute | solution.py:314
  38.4 1.6 collective-permute-start.3
  40.0 2.5 %collective-permute-start.4 = (bf16[32,1152]{1,0:T(8,128)(2,1)}, bf16[32,1152]{1,0:T(8,128)(2,1)S(1)}, u32[]{:S(2)}, u32[]{:S(2)}) collective-permute-start(bf16[32,1152]{1,0:T(8,128)(2,1)} %copy-done.15), channel_id=1, source_target_pairs={{0,160},{32,192},{64,224},{96,0},{128,32},{160,64},{192,96},{224,1... | collective-permute-start | bytes 221192 | tf_op jit(solution)/shard_map/ppermute | solution.py:314
  42.5 0.9 collective-permute-done.1.refs_2_
  43.5 0.1 pad_add_fusion.place_ref
  43.5 2.8 %collective-permute-done.2.refs_3_ = bf16[32,1152]{1,0:T(8,128)(2,1)S(1)} collective-permute-done((bf16[32,1152]{1,0:T(8,128)(2,1)}, bf16[32,1152]{1,0:T(8,128)(2,1)S(1)}, u32[]{:S(2)}, u32[]{:S(2)}) %collective-permute-start.2) | collective-permute-done | bytes 73760 | tf_op jit(solution)/shard_map/ppermute | solution.py:314
  46.4 0.0 collective-permute-done.3.refs_4_
  46.4 0.0 collective-permute-done.4.refs_5_
  46.4 0.6 collective-permute-done.5.refs_6_
  47.0 0.8 collective-permute-done.6.refs_7_
  47.8 1.1 copy-done.5
  48.8 5.2 %attend.1 = (bf16[8,36864]{1,0:T(8,128)(2,1)}, bf16[8,32768]{1,0:T(8,128)(2,1)}) custom-call(s32[8]{0:T(128)S(1)} %compare_select_fusion.source_ref, s32[8]{0:T(128)S(1)} %copy-done.13, f32[8,1152]{1,0:T(8,128)S(1)} %maximum_convert_fusion.new_ref, bf16[8,36864]{1,0:T(8,128)(2,1)S(1)} %copy-done.5, bf16[32,1152]{1,0:T(8,128)(2,1)S(1)} %get-tuple-element.19.refs_0_, ...), custom_call_target="tpu_custom_call" | custom-call | tf_op jit(solution)/shard_map/attend/pallas_call | solution.py:319
  54.0 7.9 %all-to-all-done.1.rows_ref = bf16[32,24,896]{2,1,0:T(8,128)(2,1)S(1)} async-done(((bf16[32,24,896]{2,1,0:T(8,128)(2,1)}), bf16[32,24,896]{2,1,0:T(8,128)(2,1)S(1)}, u32[]{:S(2)}, u32[]{:S(2)}) %all-to-all-start.1) | async-done | bytes 1376288 | tf_op jit(solution)/shard_map/all_to_all | solution.py:335
  61.9 1.5 copy-done.1
  63.4 1.1 copy-done.3
  64.5 2.8 %partial.2.refs_0_ = bf16[2,384,1024]{2,1,0:T(8,128)(2,1)S(1)} custom-call(s32[2]{0:T(128)S(1)} %pad_add_fusion.place_ref, bf16[32,24,896]{2,1,0:T(8,128)(2,1)S(1)} %all-to-all-done.1.rows_ref, bf16[896,1024]{1,0:T(8,128)(2,1)S(1)} %bitcast.5, bf16[896,1024]{1,0:T(8,128)(2,1)S(1)} %bitcast.7, bf16[8,36864]{1,0:T(8,128)(2,1)S(1)} %copy-done.3), custom_call_target="tpu_custom_call" | custom-call | tf_op jit(solution)/shard_map/partial/pallas_call | solution.py:343
  67.3 3.3 %collective-permute-start.7 = (bf16[2,384,1024]{2,1,0:T(8,128)(2,1)S(1)}, bf16[2,384,1024]{2,1,0:T(8,128)(2,1)S(1)}, u32[]{:S(2)}, u32[]{:S(2)}) collective-permute-start(bf16[2,384,1024]{2,1,0:T(8,128)(2,1)S(1)} %partial.2.refs_0_), channel_id=1, source_target_pairs={{0,32},{32,0},{64,96},{96,64},{128,160},{160,128},{192,224},{224,1... | collective-permute-start | bytes 4718600 | tf_op jit(solution)/shard_map/ppermute | solution.py:364
  70.6 2.8 %partial.3.keep_ref = bf16[2,384,1024]{2,1,0:T(8,128)(2,1)S(1)} custom-call(s32[2]{0:T(128)S(1)} %pad_add_fusion.place_ref, bf16[32,24,896]{2,1,0:T(8,128)(2,1)S(1)} %all-to-all-done.1.rows_ref, bf16[896,1024]{1,0:T(8,128)(2,1)S(1)} %bitcast.6, bf16[896,1024]{1,0:T(8,128)(2,1)S(1)} %bitcast.8, bf16[2,384,1024]{2,1,0:T(8,128)(2,1)S(1)} %partial.2.refs_0_), custom_call_target="tpu_custom_call" | custom-call | tf_op jit(solution)/shard_map/partial/pallas_call | solution.py:343
  73.4 0.3 collective-permute-done.7.got_ref
  73.6 0.9 pair.1
  74.5 0.4 collective-permute-start.8
  74.9 1.8 %collective-permute-start.9 = (bf16[2,96,1024]{2,1,0:T(8,128)(2,1)S(1)}, bf16[2,96,1024]{2,1,0:T(8,128)(2,1)S(1)}, u32[]{:S(2)}, u32[]{:S(2)}) collective-permute-start(bf16[2,96,1024]{2,1,0:T(8,128)(2,1)S(1)} %get-tuple-element.33), channel_id=1, source_target_pairs={{0,128},{32,160},{64,192},{96,224},{128,0},{160,32},{192,64},{224,... | collective-permute-start | bytes 1179656 | tf_op jit(solution)/shard_map/ppermute | solution.py:372
  76.7 0.8 collective-permute-start.10
  77.5 9.3 %collective-permute-done.8.refs_0_ = bf16[2,96,1024]{2,1,0:T(8,128)(2,1)S(1)} collective-permute-done((bf16[2,96,1024]{2,1,0:T(8,128)(2,1)S(1)}, bf16[2,96,1024]{2,1,0:T(8,128)(2,1)S(1)}, u32[]{:S(2)}, u32[]{:S(2)}) %collective-permute-start.8) | collective-permute-done | bytes 393248 | tf_op jit(solution)/shard_map/ppermute | solution.py:372
  86.8 7.3 %collective-permute-done.9.refs_1_ = bf16[2,96,1024]{2,1,0:T(8,128)(2,1)S(1)} collective-permute-done((bf16[2,96,1024]{2,1,0:T(8,128)(2,1)S(1)}, bf16[2,96,1024]{2,1,0:T(8,128)(2,1)S(1)}, u32[]{:S(2)}, u32[]{:S(2)}) %collective-permute-start.9) | collective-permute-done | bytes 393248 | tf_op jit(solution)/shard_map/ppermute | solution.py:372
  94.0 0.9 collective-permute-done.10.refs_2_
  94.9 0.3 units.1.refs_0_
  95.2 1.2 collective-permute-start.13
  96.4 3.2 %collective-permute-start.12 = (bf16[96,1024]{1,0:T(8,128)(2,1)S(1)}, bf16[96,1024]{1,0:T(8,128)(2,1)S(1)}, u32[]{:S(2)}, u32[]{:S(2)}) collective-permute-start(bf16[96,1024]{1,0:T(8,128)(2,1)S(1)} %units.1.refs_0_), channel_id=1, source_target_pairs={{0,128},{32,160},{64,192},{96,224},{128,0},{160,32},{192,64},{224,... | collective-permute-start | bytes 589832 | tf_op jit(solution)/shard_map/ppermute | solution.py:374
  99.5 0.0 collective-permute-start.11
  99.5 2.7 %collective-permute-done.13.refs_3_ = bf16[96,1024]{1,0:T(8,128)(2,1)S(1)} collective-permute-done((bf16[96,1024]{1,0:T(8,128)(2,1)S(1)}, bf16[96,1024]{1,0:T(8,128)(2,1)S(1)}, u32[]{:S(2)}, u32[]{:S(2)}) %collective-permute-start.13) | collective-permute-done | bytes 196640 | tf_op jit(solution)/shard_map/ppermute | solution.py:374
  102.2 5.9 %collective-permute-done.12.refs_2_ = bf16[96,1024]{1,0:T(8,128)(2,1)S(1)} collective-permute-done((bf16[96,1024]{1,0:T(8,128)(2,1)S(1)}, bf16[96,1024]{1,0:T(8,128)(2,1)S(1)}, u32[]{:S(2)}, u32[]{:S(2)}) %collective-permute-start.12) | collective-permute-done | bytes 196640 | tf_op jit(solution)/shard_map/ppermute | solution.py:374
  108.1 0.0 collective-permute-done.11.refs_1_
  108.1 0.1 pad_maximum_fusion
  108.2 1.6 collective-permute-start.14
  109.7 1.9 %collective-permute-done.14.refs_4_ = bf16[384,1024]{1,0:T(8,128)(2,1)S(1)} collective-permute-done((bf16[384,1024]{1,0:T(8,128)(2,1)S(1)}, bf16[384,1024]{1,0:T(8,128)(2,1)S(1)}, u32[]{:S(2)}, u32[]{:S(2)}) %collective-permute-start.14) | collective-permute-done | bytes 786464 | tf_op jit(solution)/shard_map/ppermute | solution.py:375
  111.7 2.3 %down.1 = bf16[32,24,896]{2,1,0:T(8,128)(2,1)S(1)} custom-call(s32[2]{0:T(128)S(1)} %pad_add_fusion.place_ref, bf16[96,1024]{1,0:T(8,128)(2,1)S(1)} %units.1.refs_0_, bf16[96,1024]{1,0:T(8,128)(2,1)S(1)} %collective-permute-done.11.refs_1_, bf16[96,1024]{1,0:T(8,128)(2,1)S(1)} %collective-permute-done.12.refs_2_, ...), custom_call_target="tpu_custom_call" | custom-call | tf_op jit(solution)/shard_map/down/pallas_call | solution.py:376
  114.0 40.8 %all_to_all.21.refs_1_ = bf16[32,24,896]{2,1,0:T(8,128)(2,1)S(1)} all-to-all(bf16[32,24,896]{2,1,0:T(8,128)(2,1)S(1)} %down.1), channel_id=1, replica_groups=mesh['req'=8,'exp'=32] {'exp'}, dimensions={0} | all-to-all | bytes 2752512 | tf_op jit(solution)/shard_map/all_to_all | solution.py:382
  154.8 0.6 combine.1
  155.4 10.6 %all_to_all.22.parts_ref = bf16[8,8,896]{2,1,0:T(8,128)(2,1)S(1)} all-to-all(bf16[8,8,896]{2,1,0:T(8,128)(2,1)S(1)} %combine.1), channel_id=1, replica_groups=mesh['req'=8,'exp'=32] {'req'}, dimensions={0} | all-to-all | bytes 229376 | tf_op jit(solution)/shard_map/all_to_all | solution.py:387
  166.0 0.7 spread.1
  (27 shorter events, 0.1 us)
Async XLA Ops:
  0.6 0.9 copy-start.8
  1.5 0.7 copy-start.9
  2.2 0.7 copy-start.10
  2.9 0.7 copy-start.11
  4.3 25.0 %copy-start.18 = (bf16[8,576]{1,0:T(8,128)(2,1)S(1)}, bf16[8,576]{1,0:T(8,128)(2,1)}, u32[]{:S(2)}) copy-start(bf16[8,576]{1,0:T(8,128)(2,1)} %param.14) | copy-start | bytes 27652
  17.3 0.8 copy-start.6
  18.1 18.1 %copy-start.12 = (s32[8]{0:T(128)S(1)}, s32[8]{0:T(128)}, u32[]{:S(2)}) copy-start(s32[8]{0:T(128)} %slot_ref.1) | copy-start | bytes 100
  18.1 29.7 %copy-start.13 = (s32[8]{0:T(128)S(1)}, s32[8]{0:T(128)}, u32[]{:S(2)}) copy-start(s32[8]{0:T(128)} %length_ref.1) | copy-start | bytes 100
  18.1 43.8 %all-to-all-start.1 = ((bf16[32,24,896]{2,1,0:T(8,128)(2,1)}), bf16[32,24,896]{2,1,0:T(8,128)(2,1)S(1)}, u32[]{:S(2)}, u32[]{:S(2)}) async-start(bf16[32,24,896]{2,1,0:T(8,128)(2,1)} %get-tuple-element.30), calls=%async_computation.1 | async-start | bytes 2752512 | tf_op jit(solution)/shard_map/all_to_all | solution.py:335
  29.3 32.7 %copy-start = (bf16[1,896,1024]{2,1,0:T(8,128)(2,1)S(1)}, bf16[1,896,1024]{2,1,0:T(8,128)(2,1)}, u32[]{:S(2)}) copy-start(bf16[1,896,1024]{2,1,0:T(8,128)(2,1)} %param.19) | copy-start | bytes 5505028
  29.8 1.1 copy-start.4
  32.4 0.6 copy-start.14
  33.0 0.6 copy-start.15
  33.6 0.6 copy-start.16
  34.3 0.6 copy-start.17
  34.9 7.6 %collective-permute-start = (bf16[32,1152]{1,0:T(8,128)(2,1)}, bf16[32,1152]{1,0:T(8,128)(2,1)S(1)}, u32[]{:S(2)}, u32[]{:S(2)}) collective-permute-start(bf16[32,1152]{1,0:T(8,128)(2,1)} %get-tuple-element.20), channel_id=1, source_target_pairs={{0,32},{32,64},{64,96},{96,128},{128,160},{160,192},{192,224},{224... | collective-permute-start | bytes 221192 | tf_op jit(solution)/shard_map/ppermute | solution.py:314
  36.2 7.3 %collective-permute-start.1 = (bf16[32,1152]{1,0:T(8,128)(2,1)}, bf16[32,1152]{1,0:T(8,128)(2,1)S(1)}, u32[]{:S(2)}, u32[]{:S(2)}) collective-permute-start(bf16[32,1152]{1,0:T(8,128)(2,1)} %get-tuple-element.21), channel_id=1, source_target_pairs={{0,64},{32,96},{64,128},{96,160},{128,192},{160,224},{192,0},{224,... | collective-permute-start | bytes 221192 | tf_op jit(solution)/shard_map/ppermute | solution.py:314
  36.3 10.1 %collective-permute-start.2 = (bf16[32,1152]{1,0:T(8,128)(2,1)}, bf16[32,1152]{1,0:T(8,128)(2,1)S(1)}, u32[]{:S(2)}, u32[]{:S(2)}) collective-permute-start(bf16[32,1152]{1,0:T(8,128)(2,1)} %copy-done.17), channel_id=1, source_target_pairs={{0,96},{32,128},{64,160},{96,192},{128,224},{160,0},{192,32},{224,... | collective-permute-start | bytes 221192 | tf_op jit(solution)/shard_map/ppermute | solution.py:314
  38.4 8.0 %collective-permute-start.3 = (bf16[32,1152]{1,0:T(8,128)(2,1)}, bf16[32,1152]{1,0:T(8,128)(2,1)S(1)}, u32[]{:S(2)}, u32[]{:S(2)}) collective-permute-start(bf16[32,1152]{1,0:T(8,128)(2,1)} %copy-done.16), channel_id=1, source_target_pairs={{0,128},{32,160},{64,192},{96,224},{128,0},{160,32},{192,64},{224,... | collective-permute-start | bytes 221192 | tf_op jit(solution)/shard_map/ppermute | solution.py:314
  40.0 6.4 %collective-permute-start.4 = (bf16[32,1152]{1,0:T(8,128)(2,1)}, bf16[32,1152]{1,0:T(8,128)(2,1)S(1)}, u32[]{:S(2)}, u32[]{:S(2)}) collective-permute-start(bf16[32,1152]{1,0:T(8,128)(2,1)} %copy-done.15), channel_id=1, source_target_pairs={{0,160},{32,192},{64,224},{96,0},{128,32},{160,64},{192,96},{224,1... | collective-permute-start | bytes 221192 | tf_op jit(solution)/shard_map/ppermute | solution.py:314
  42.5 4.5 %collective-permute-start.5 = (bf16[32,1152]{1,0:T(8,128)(2,1)}, bf16[32,1152]{1,0:T(8,128)(2,1)S(1)}, u32[]{:S(2)}, u32[]{:S(2)}) collective-permute-start(bf16[32,1152]{1,0:T(8,128)(2,1)} %copy-done.14), channel_id=1, source_target_pairs={{0,192},{32,224},{64,0},{96,32},{128,64},{160,96},{192,128},{224,1... | collective-permute-start | bytes 221192 | tf_op jit(solution)/shard_map/ppermute | solution.py:314
  43.5 4.3 %collective-permute-start.6 = (bf16[32,1152]{1,0:T(8,128)(2,1)S(1)}, bf16[32,1152]{1,0:T(8,128)(2,1)S(1)}, u32[]{:S(2)}, u32[]{:S(2)}) collective-permute-start(bf16[32,1152]{1,0:T(8,128)(2,1)S(1)} %get-tuple-element.26), channel_id=1, source_target_pairs={{0,224},{32,0},{64,32},{96,64},{128,96},{160,128},{192,160},{224,1... | collective-permute-start | bytes 221192 | tf_op jit(solution)/shard_map/ppermute | solution.py:314
  47.8 1.1 copy-start.5
  61.9 1.5 copy-start.1
  63.4 1.1 copy-start.3
  67.3 6.4 %collective-permute-start.7 = (bf16[2,384,1024]{2,1,0:T(8,128)(2,1)S(1)}, bf16[2,384,1024]{2,1,0:T(8,128)(2,1)S(1)}, u32[]{:S(2)}, u32[]{:S(2)}) collective-permute-start(bf16[2,384,1024]{2,1,0:T(8,128)(2,1)S(1)} %partial.2.refs_0_), channel_id=1, source_target_pairs={{0,32},{32,0},{64,96},{96,64},{128,160},{160,128},{192,224},{224,1... | collective-permute-start | bytes 4718600 | tf_op jit(solution)/shard_map/ppermute | solution.py:364
  74.5 12.2 %collective-permute-start.8 = (bf16[2,96,1024]{2,1,0:T(8,128)(2,1)S(1)}, bf16[2,96,1024]{2,1,0:T(8,128)(2,1)S(1)}, u32[]{:S(2)}, u32[]{:S(2)}) collective-permute-start(bf16[2,96,1024]{2,1,0:T(8,128)(2,1)S(1)} %get-tuple-element.32), channel_id=1, source_target_pairs={{0,64},{32,96},{64,128},{96,160},{128,192},{160,224},{192,0},{224,... | collective-permute-start | bytes 1179656 | tf_op jit(solution)/shard_map/ppermute | solution.py:372
  74.9 19.1 %collective-permute-start.9 = (bf16[2,96,1024]{2,1,0:T(8,128)(2,1)S(1)}, bf16[2,96,1024]{2,1,0:T(8,128)(2,1)S(1)}, u32[]{:S(2)}, u32[]{:S(2)}) collective-permute-start(bf16[2,96,1024]{2,1,0:T(8,128)(2,1)S(1)} %get-tuple-element.33), channel_id=1, source_target_pairs={{0,128},{32,160},{64,192},{96,224},{128,0},{160,32},{192,64},{224,... | collective-permute-start | bytes 1179656 | tf_op jit(solution)/shard_map/ppermute | solution.py:372
  76.7 18.2 %collective-permute-start.10 = (bf16[2,96,1024]{2,1,0:T(8,128)(2,1)S(1)}, bf16[2,96,1024]{2,1,0:T(8,128)(2,1)S(1)}, u32[]{:S(2)}, u32[]{:S(2)}) collective-permute-start(bf16[2,96,1024]{2,1,0:T(8,128)(2,1)S(1)} %get-tuple-element.34), channel_id=1, source_target_pairs={{0,192},{32,224},{64,0},{96,32},{128,64},{160,96},{192,128},{224,1... | collective-permute-start | bytes 1179656 | tf_op jit(solution)/shard_map/ppermute | solution.py:372
  94.9 16.7 %copy-start.2 = (bf16[1,1024,896]{2,1,0:T(8,128)(2,1)S(1)}, bf16[1,1024,896]{2,1,0:T(8,128)(2,1)}, u32[]{:S(2)}) copy-start(bf16[1,1024,896]{2,1,0:T(8,128)(2,1)} %param.21) | copy-start | bytes 5505028
  95.2 7.0 %collective-permute-start.13 = (bf16[96,1024]{1,0:T(8,128)(2,1)S(1)}, bf16[96,1024]{1,0:T(8,128)(2,1)S(1)}, u32[]{:S(2)}, u32[]{:S(2)}) collective-permute-start(bf16[96,1024]{1,0:T(8,128)(2,1)S(1)} %units.1.refs_0_), channel_id=1, source_target_pairs={{0,64},{32,96},{64,128},{96,160},{128,192},{160,224},{192,0},{224,... | collective-permute-start | bytes 589832 | tf_op jit(solution)/shard_map/ppermute | solution.py:374
  96.4 11.7 %collective-permute-start.12 = (bf16[96,1024]{1,0:T(8,128)(2,1)S(1)}, bf16[96,1024]{1,0:T(8,128)(2,1)S(1)}, u32[]{:S(2)}, u32[]{:S(2)}) collective-permute-start(bf16[96,1024]{1,0:T(8,128)(2,1)S(1)} %units.1.refs_0_), channel_id=1, source_target_pairs={{0,128},{32,160},{64,192},{96,224},{128,0},{160,32},{192,64},{224,... | collective-permute-start | bytes 589832 | tf_op jit(solution)/shard_map/ppermute | solution.py:374
  99.5 8.6 %collective-permute-start.11 = (bf16[96,1024]{1,0:T(8,128)(2,1)S(1)}, bf16[96,1024]{1,0:T(8,128)(2,1)S(1)}, u32[]{:S(2)}, u32[]{:S(2)}) collective-permute-start(bf16[96,1024]{1,0:T(8,128)(2,1)S(1)} %units.1.refs_0_), channel_id=1, source_target_pairs={{0,192},{32,224},{64,0},{96,32},{128,64},{160,96},{192,128},{224,1... | collective-permute-start | bytes 589832 | tf_op jit(solution)/shard_map/ppermute | solution.py:374
  108.2 3.5 %collective-permute-start.14 = (bf16[384,1024]{1,0:T(8,128)(2,1)S(1)}, bf16[384,1024]{1,0:T(8,128)(2,1)S(1)}, u32[]{:S(2)}, u32[]{:S(2)}) collective-permute-start(bf16[384,1024]{1,0:T(8,128)(2,1)S(1)} %pad_maximum_fusion), channel_id=1, source_target_pairs={{0,32},{32,0},{64,96},{96,64},{128,160},{160,128},{192,224},{224,1... | collective-permute-start | bytes 2359304 | tf_op jit(solution)/shard_map/ppermute | solution.py:375
  114.0 40.8 %copy-start.7 = (bf16[2,768,64]{2,1,0:T(8,128)(2,1)S(1)}, bf16[2,768,64]{2,1,0:T(8,128)(2,1)}, u32[]{:S(2)}) copy-start(bf16[2,768,64]{2,1,0:T(8,128)(2,1)} %copy-done.6) | copy-start | bytes 589828

commit v2 on v1

v2 whole, which is shorter than its diff:
```python
import functools

import jax
import jax.numpy as jnp
from jax import lax
from jax.experimental import pallas as pl
from jax.experimental.pallas import tpu as pltpu
from jax.sharding import PartitionSpec as P

LAT = 512
CAP = 3
CORES = 2
NOTE = 128
ROUTE, PART, DOWN, TILES = 32, 58, 32, 2

score_scale = 0.07216878364870323

VMEM = pl.BlockSpec(memory_space=pltpu.VMEM)
SMEM = pl.BlockSpec(memory_space=pltpu.SMEM)
ANY = pl.BlockSpec(memory_space=pl.ANY)
MIB = 1024 * 1024
BF = jnp.bfloat16
F32 = jnp.float32


def iota(shape, axis):
    return lax.broadcasted_iota(jnp.int32, shape, axis)


def dot(a, b, contract=((1,), (0,))):
    return lax.dot_general(a, b, (contract, ((), ())), preferred_element_type=F32)


def shape_of(shape, dtype=BF):
    return jax.ShapeDtypeStruct(shape, dtype)


def announce_kernel(column_span, *refs):
    sources, out_ref, targets, sems = refs[:4], refs[4], refs[5:9], refs[9]
    copies = [pltpu.make_async_copy(a, b, sems.at[i]) for i, (a, b) in enumerate(zip(sources, targets))]
    for copy in copies:
        copy.start()
    for copy in copies:
        copy.wait()
    slot_ref, hidden_ref, ids_ref, gates_ref = targets
    ring, rows, width = out_ref.shape
    part = width - NOTE
    top = ids_ref.shape[1]
    lane = iota((rows, NOTE), 1)
    gates = gates_ref[...]
    first = gates.astype(BF).astype(F32)
    second = (gates - first).astype(BF).astype(F32)
    third = gates - first - second
    note = jnp.zeros((rows, NOTE), F32)
    for group, values in enumerate((ids_ref[...].astype(F32), first, second, third)):
        for k in range(top):
            note = jnp.where(lane == group * top + k, values[:, k : k + 1], note)
    for chip in range(ring):
        own = note
        for core in range(CORES):
            wanted = jnp.int32(0)
            for j in range(rows):
                slot = slot_ref[j]
                same = slot // column_span == chip * CORES + core
                wanted += jnp.where(same, slot % rows, 0)
            own = jnp.where(lane == 4 * top + core, wanted.astype(F32), own)
        out_ref[chip, :, 0:part] = hidden_ref[:, chip * part : (chip + 1) * part]
        out_ref[chip, :, part:width] = own.astype(BF)


def routing(top, experts, arrived_ref):
    blocks, rows, width = arrived_ref.shape
    tokens = blocks * rows
    stacked = jnp.concatenate([arrived_ref[b].astype(F32) for b in range(blocks)], axis=0)
    note = stacked[:, width - NOTE : width]
    note = jnp.concatenate([note, jnp.zeros((NOTE - tokens, NOTE), F32)], axis=0).T[:, 0:tokens]
    expert = iota((experts, tokens), 0).astype(F32)
    member = jnp.zeros((experts, tokens), F32)
    gate = jnp.zeros((experts, tokens), F32)
    for k in range(top):
        hit = note[k : k + 1, :] == expert
        value = note[top + k : top + k + 1, :] + note[2 * top + k : 2 * top + k + 1, :]
        value = value + note[3 * top + k : 3 * top + k + 1, :]
        member = jnp.where(hit, 1.0, member)
        gate = jnp.where(hit, value, gate)
    one, two = iota((tokens, tokens), 0), iota((tokens, tokens), 1)
    before = jnp.where((one // rows == two // rows) & (one < two), 1.0, 0.0).astype(BF)
    rank = dot(member.astype(BF), before)
    place = rank * blocks + (iota((experts, tokens), 1) // rows).astype(F32)
    place = jnp.where(member > 0.5, place, -1.0)
    slots = CAP * blocks
    row = iota((experts, CORES * slots, tokens), 1)

    def slots_of(half, factor):
        wanted = jnp.where(row // slots == half, row % slots, -2).astype(F32)
        taken = jnp.where(wanted == place[:, None, :], factor, 0.0)
        return taken.reshape(experts * CORES * slots, tokens)

    return stacked[:, 0 : width - NOTE].astype(BF), gate[:, None, :], slots_of


def route_kernel(top, arrived_ref, out_ref):
    features, _, slots_of = routing(top, out_ref.shape[0], arrived_ref)
    part = features.shape[1] // CORES
    total = 0.0
    for half in range(CORES):
        own = features[:, half * part : (half + 1) * part]
        total = total + dot(slots_of(half, 1.0).astype(BF), own)
    out_ref[...] = total.reshape(out_ref.shape).astype(BF)


def weigh_kernel(top, experts, arrived_ref, out_ref):
    _, gate, slots_of = routing(top, experts, arrived_ref)
    weigh = [slots_of(half, gate) for half in range(CORES)]
    high = [w.astype(BF).astype(F32) for w in weigh]
    low = [w - h for w, h in zip(weigh, high)]
    out_ref[...] = jnp.concatenate(high + low, axis=1).astype(BF)


def half_select(core, count, slots):
    size = count * slots
    row = iota((CORES * size, 1), 0)
    half = jnp.where(row < size, core, 1 - core)
    target = (row % size) // slots * CORES * slots + half * slots + row % slots
    column = iota((CORES * size, CORES * size), 1)
    return jnp.where(column == target, 1.0, 0.0).astype(BF)


def write_sums(own_ref, other_ref, weight_ref, weight2_ref, out_refs):
    size = out_refs[0].shape[0]
    result = dot(own_ref[...], weight_ref[...]) + dot(other_ref[...], weight2_ref[...])
    for d, out_ref in enumerate(out_refs):
        out_ref[...] = result[d * size : (d + 1) * size].astype(out_ref.dtype)


def gate_kernel(place_ref, rows_ref, gate_ref, gate2_ref, *refs):
    own_ref, other_ref, out_refs = refs[0], refs[1], refs[2:]
    ring, size = len(out_refs), out_refs[0].shape[0]
    sources, double, part = rows_ref.shape
    count = sources // ring

    @pl.when(pl.program_id(0) == 0)
    def _():
        select = half_select(place_ref[1], count, double // CORES)
        for d in range(ring):
            start = lax.rem(place_ref[0] + d, ring) * count
            rows = rows_ref[pl.ds(start, count)].astype(F32)
            both = dot(select, rows.reshape(count * double, part).astype(BF)).astype(BF)
            own_ref[d * size : (d + 1) * size, :] = both[0:size]
            other_ref[d * size : (d + 1) * size, :] = both[size:]

    write_sums(own_ref, other_ref, gate_ref, gate2_ref, out_refs)


def up_kernel(own_ref, other_ref, up_ref, up2_ref, *out_refs):
    write_sums(own_ref, other_ref, up_ref, up2_ref, out_refs)


def units_kernel(*refs):
    part_refs, out_ref = refs[:-1], refs[-1]
    gate, up = (sum(ref[...].astype(F32) for ref in part_refs[i::2]) for i in range(2))
    units = (gate / (1.0 + jnp.exp(-gate)) * up).astype(BF)
    for d in range(out_ref.shape[0]):
        out_ref[d] = units


def down_kernel(place_ref, units_ref, weight_ref, weight2_ref, out_ref):
    ring, size, inner = units_ref.shape
    sources, double, part = out_ref.shape
    count = sources // ring
    rows = jnp.concatenate([units_ref[d] for d in range(ring)], axis=0)
    own = dot(rows, weight_ref[...]).astype(BF)
    other = dot(rows, weight2_ref[...]).astype(BF)
    select = half_select(place_ref[1], count, double // CORES)
    for d in range(ring):
        piece = slice(d * size, (d + 1) * size)
        both = dot(select, jnp.concatenate([own[piece], other[piece]], axis=0), ((0,), (0,)))
        out_ref[d * count : (d + 1) * count] = both.reshape(count, double, part).astype(BF)


def combine_kernel(weights_ref, result_ref, out_ref):
    experts, double, part = result_ref.shape
    ring, rows, _ = out_ref.shape
    results = result_ref[...].astype(F32).reshape(experts * double, part).astype(BF)
    sums = dot(weights_ref[...], results, ((0,), (0,)))
    tokens = ring * rows
    for half in range(CORES):
        total = sums[half * tokens : (half + 1) * tokens]
        total = total + sums[(CORES + half) * tokens : (CORES + half + 1) * tokens]
        out_ref[:, :, half * part : (half + 1) * part] = total.reshape(ring, rows, part).astype(BF)


def spread_kernel(parts_ref, out_ref):
    peers, _, part = parts_ref.shape
    for peer in range(peers):
        out_ref[:, peer * part : (peer + 1) * part] = parts_ref[peer]


def stack_pairs(flat_ref, stacked_ref):
    rows = flat_ref.shape[0]
    total, span = stacked_ref.shape
    for p in range(0, total // rows, 2):
        both = [flat_ref[:, q * span : (q + 1) * span].astype(F32) for q in (p, p + 1)]
        stacked_ref[p * rows : (p + 2) * rows, :] = jnp.concatenate(both, axis=0).astype(BF)


def unstack_pairs(stacked, flat_ref):
    rows = flat_ref.shape[0]
    total, span = stacked.shape
    for p in range(total // rows):
        flat_ref[:, p * span : (p + 1) * span] = stacked[p * rows : (p + 1) * rows].astype(BF)


def pack_kernel(asked_ref, cache_ref, *refs):
    out_refs, stacked_ref = refs[:-1], refs[-1]
    rows = len(out_refs)
    pairs, span = out_refs[0].shape
    stack_pairs(cache_ref, stacked_ref)
    pair, column = iota((pairs, pairs * rows), 0), iota((pairs, pairs * rows), 1)
    same_pair = column // rows == pair
    select = [
        jnp.where(same_pair & (column % rows == asked_ref[r]), 1.0, 0.0) for r in range(rows)
    ]
    select = jnp.concatenate(select, axis=0).astype(BF)
    packed = dot(select, stacked_ref[...])
    for r, out_ref in enumerate(out_refs):
        out_ref[...] = packed[r * pairs : (r + 1) * pairs].astype(BF)


def attend_kernel(
    source_ref, length_ref, new_ref, queries_ref, *refs
):
    cache_ref, mixed_ref, token_ref, arrived_ref, stacked_ref, keys_ref, out_ref = refs[-7:]
    token_ref[...] = jnp.zeros(token_ref.shape, F32)
    rows, pairs, span = arrived_ref.shape
    for d, moved_ref in enumerate(refs[:-7]):
        arrived_ref[d] = moved_ref[...].astype(F32)
    width = span // 2
    reach = -(-width // 128) * 128
    total = rows * pairs
    one, two = iota((total, total), 0), iota((total, total), 1)
    to_rows = (one // pairs == two % rows) & (one % pairs == two // rows)
    to_rows = jnp.where(to_rows, 1.0, 0.0).astype(BF)
    to_pairs = (one // rows == two % pairs) & (one % rows == two // pairs)
    to_pairs = jnp.where(to_pairs, 1.0, 0.0).astype(BF)
    stack_pairs(queries_ref, stacked_ref)
    queries = dot(to_rows, stacked_ref[...])
    turned = pltpu.roll(queries, width, 1)
    inside = iota((2 * pairs, reach), 1) < width
    pair, lane = iota((pairs, span), 0), iota((pairs, span), 1)
    column = iota((2 * pairs, 2 * pairs), 1)
    position = 2 * (column % pairs) + column // pairs
    for j in range(rows):
        length = length_ref[j]
        keys = arrived_ref[source_ref[j]]
        placed = (pair == length // 2) & ((lane >= width) == (length % 2 == 1))
        keys = jnp.where(placed, new_ref[j : j + 1, :], keys)
        keys_ref[j * pairs : (j + 1) * pairs, :] = keys.astype(BF)
        both = jnp.concatenate([keys, pltpu.roll(keys, width, 1)], axis=0)[:, 0:reach].astype(BF)
        own = slice(j * pairs, (j + 1) * pairs)
        heads = jnp.concatenate([queries[own, 0:reach], turned[own, 0:reach]], axis=0)
        heads = jnp.where(inside, heads, 0.0).astype(BF)
        scores = dot(heads, both, ((1,), (1,))) * score_scale
        scores = jnp.where(position <= length, scores, -jnp.inf)
        raised = jnp.exp(scores - jnp.max(scores, axis=1, keepdims=True))
        weights = (raised / jnp.sum(raised, axis=1, keepdims=True)).astype(BF)
        mixed = dot(weights, both[:, 0:LAT])
        mixed = jnp.concatenate([mixed[0:pairs], mixed[pairs:]], axis=1)
        out_ref[j * pairs : (j + 1) * pairs, :] = mixed.astype(BF)
    unstack_pairs(dot(to_pairs, keys_ref[...]), cache_ref)
    unstack_pairs(dot(to_pairs, out_ref[...]), mixed_ref)


def call(kernel, out_shape, in_specs, name, scratch=(), after=(), limit=32):
    count = len(in_specs)

    def body(*refs):
        kernel(*refs[:count], *refs[count + len(after) :])

    return lambda *args: pl.pallas_call(
        body,
        out_shape=out_shape,
        in_specs=in_specs + [VMEM] * len(after),
        out_specs=jax.tree.map(lambda _: VMEM, out_shape),
        scratch_shapes=list(scratch),
        compiler_params=pltpu.CompilerParams(vmem_limit_bytes=limit * MIB),
        name=name,
    )(*args, *after)


TOKEN = jax.ShapeDtypeStruct((8, 128), F32)


def on_device(
    latent_cache,
    old_slot,
    lengths,
    new_latent,
    queries,
    hidden,
    expert_ids,
    expert_gates,
    gate_weight,
    up_weight,
    down_weight,
):
    rows, features = hidden.shape
    top = expert_ids.shape[1]
    peers = lax.axis_size("req")
    experts = lax.axis_size("exp")
    ring = peers // CORES
    part = features // ring
    inner = gate_weight.shape[2]
    me = lax.axis_index("req").astype(jnp.int32)
    place = jnp.stack([me // CORES, me % CORES])
    swap = [(k, k ^ 1) for k in range(peers)]
    same_core = [[k for k in range(peers) if k % CORES == c] for c in range(CORES)]

    def along(d):
        return [(k, (k + CORES * d) % peers) for k in range(peers)]

    def exchange_y(x):
        return lax.all_to_all(
            x, "req", split_axis=0, concat_axis=0, tiled=True, axis_index_groups=same_core
        )

    column_span = experts * rows
    message = call(
        functools.partial(announce_kernel, column_span),
        shape_of((ring, rows, part + NOTE)),
        [ANY] * 4,
        "announce",
        [
            pltpu.SMEM(old_slot.shape, jnp.int32),
            pltpu.VMEM(hidden.shape, BF),
            pltpu.VMEM(expert_ids.shape, jnp.int32),
            pltpu.VMEM(expert_gates.shape, F32),
            pltpu.SemaphoreType.DMA((4,)),
        ],
        limit=56,
    )(old_slot, hidden, expert_ids, expert_gates)
    arrived = exchange_y(message)

    own_weights = [w[0] for w in (gate_weight, up_weight, down_weight)]
    sibling_weights = [lax.ppermute(w, "req", swap) for w in own_weights]

    width = new_latent.shape[1]
    span = 2 * width
    pairs = latent_cache.shape[1] // span
    asked = arrived[:, 0, part + 4 * top : part + 4 * top + CORES].astype(jnp.int32)
    asked = asked.T
    core = place[1]
    other = lax.ppermute(lax.dynamic_index_in_dim(asked, 1 - core, 0, False), "req", swap)
    asked = lax.dynamic_index_in_dim(asked, core, 0, False)
    asked = jnp.where(core == 0, jnp.stack([asked, other], 1), jnp.stack([other, asked], 1))
    asked = jnp.roll(asked.reshape(-1), -me)
    packed = call(
        pack_kernel,
        [shape_of((pairs, span))] * peers,
        [SMEM, VMEM],
        "pack",
        [pltpu.VMEM((rows * pairs, span), BF)],
    )(asked, latent_cache)
    moved = [packed[0]] + [
        lax.ppermute(packed[d], "req", [(k, (k + d) % peers) for k in range(peers)])
        for d in range(1, peers)
    ]
    new_pair = jnp.concatenate([new_latent, new_latent], axis=1).astype(F32)
    source = lax.rem(me - old_slot // column_span + peers, peers)
    cache_out, attention, done = call(
        attend_kernel,
        [shape_of(latent_cache.shape), shape_of((rows, pairs * 2 * LAT)), TOKEN],
        [SMEM, SMEM, VMEM, VMEM] + [VMEM] * peers,
        "attend",
        [
            pltpu.VMEM((rows, pairs, span), F32),
            pltpu.VMEM((rows * pairs, span), BF),
            pltpu.VMEM((rows * pairs, span), BF),
            pltpu.VMEM((rows * pairs, 2 * LAT), BF),
        ],
    )(source, lengths, new_pair, queries, *moved)


    slots = CAP * ring
    outgoing = call(
        functools.partial(route_kernel, top),
        shape_of((experts, CORES * slots, part // CORES)),
        [VMEM],
        "route",
        limit=ROUTE,
    )(arrived)
    received = lax.all_to_all(outgoing, "exp", split_axis=0, concat_axis=0, tiled=True)
    weights = call(
        functools.partial(weigh_kernel, top, experts),
        shape_of((experts * CORES * slots, 2 * CORES * ring * rows)),
        [VMEM],
        "weigh",
    )(arrived)

    size = experts // ring * slots
    tile = inner // TILES
    width_own = part // CORES
    column = pl.BlockSpec((width_own, tile), lambda i: (0, i))
    sums_spec = [pl.BlockSpec((size, tile), lambda i: (0, i))] * ring
    sums_shape = [shape_of((size, inner), F32)] + [shape_of((size, inner))] * (ring - 1)
    rows_spec = [pl.BlockSpec((ring * size, width_own), lambda i: (0, 0))] * 2
    params = pltpu.CompilerParams(vmem_limit_bytes=PART * MIB)
    mine, theirs, *gates = pl.pallas_call(
        lambda *refs: gate_kernel(*refs[:4], *refs[6:]),
        grid=(TILES,),
        out_shape=[shape_of((ring * size, width_own))] * 2 + sums_shape,
        in_specs=[SMEM, pl.BlockSpec(received.shape, lambda i: (0, 0, 0))] + [column] * 2 + [ANY] * 2,
        out_specs=rows_spec + sums_spec,
        compiler_params=params,
        name="gate",
    )(place, received, own_weights[0], sibling_weights[0], done, weights)
    ups = pl.pallas_call(
        up_kernel,
        grid=(TILES,),
        out_shape=sums_shape,
        in_specs=rows_spec + [column] * 2,
        out_specs=sums_spec,
        compiler_params=params,
        name="up",
    )(mine, theirs, own_weights[1], sibling_weights[1])
    sent = [gates[0], ups[0]]
    for d in range(1, ring):
        sent += [lax.ppermute(x[d], "req", along(d)) for x in (gates, ups)]
    units = call(units_kernel, shape_of((ring, size, inner)), [VMEM] * (2 * ring), "units")(*sent)
    result = call(
        down_kernel,
        shape_of(received.shape),
        [SMEM] + [VMEM] * 3,
        "down",
        limit=DOWN,
    )(place, exchange_y(units), own_weights[2], sibling_weights[2])
    returned = lax.all_to_all(result, "exp", split_axis=0, concat_axis=0, tiled=True)
    combined = call(combine_kernel, shape_of((ring, rows, part)), [VMEM] * 2, "combine")(
        weights, returned
    )
    moe_out = call(spread_kernel, shape_of((rows, features)), [VMEM], "spread")(
        exchange_y(combined)
    )

    return (cache_out, attention, moe_out)


def solution(mesh):
    in_specs = (
        P(("req", "exp"), None),
        P(("req", "exp")),
        P(("req", "exp")),
        P(("req", "exp"), None),
        P(("req", "exp"), None),
        P(("req", "exp"), None),
        P(("req", "exp"), None),
        P(("req", "exp"), None),
        P("exp", "req", None),
        P("exp", "req", None),
        P("exp", None, "req"),
    )
    out_specs = (P(("req", "exp"), None), P(("req", "exp"), None), P(("req", "exp"), None))
    return jax.shard_map(
        on_device, mesh=mesh, in_specs=in_specs, out_specs=out_specs, check_vma=False
    )
```

time: 167 us -> 160 us (0.958); the launches traced: 167 us -> 157 us
  waiting for transfers between devices: 41.3 us -> 29.7 us
  local copies, waits for them, and re-layouts: 11.3 us -> 2.87 us
  Pallas kernels: 19.6 us -> 26.5 us
  blocking collectives: 62.4 us -> 66.7 us
    ppermute x8 -> x10, waiting for transfers between devices: 28.2 us -> 8.55 us  [the longest x6 6.22 us: on_device(): sent += [lax.ppermute(x[d], 'req', along(d)) for x in (gates, ups)]]
    all_to_all x1, blocking collectives: 40.8 us -> 49.8 us  [on_device(): lax.all_to_all(result, 'exp', split_axis=0, concat_axis=0, tiled=True)]
    unnamed x38 -> x24, local copies, waits for them, and re-layouts: 11 us -> 2.3 us
    ppermute x7, waiting for transfers between devices: 5.15 us -> 12.8 us  [on_device(): lax.ppermute(packed[d], 'req', [(k, (k + d) % peers) for k in range(peers)])]
    pallas_call x11, Pallas kernels: 19.6 us -> 26.5 us  [the longest x9 16.5 us: call(): pl.pallas_call(body, out_shape=out_shape, in_specs=in_specs + [VMEM] * le...]
    all_to_all x2, blocking collectives: 21.6 us -> 16.9 us  [exchange_y(): lax.all_to_all(x, 'req', split_axis=0, concat_axis=0, tiled=True, axis_in...]
    all_to_all x1 -> x2, starting transfers between devices: 11.2 us -> 14.8 us  [the longest x1 11.3 us: on_device(): lax.all_to_all(outgoing, 'exp', split_axis=0, concat_axis=0, tiled=True)]
    ppermute x7, starting transfers between devices: 7.6 us -> 4.39 us  [on_device(): lax.ppermute(packed[d], 'req', [(k, (k + d) % peers) for k in range(peers)])]
  transfers between devices with their start and end apart: 16 -> 19, of which waited for: 12 -> 10; matrix products, arithmetic and copies ran while one was open for 0% -> 1% of each run, Pallas kernels for 6% -> 11%
where the time goes in v2:
time: 160 us; the launch traced here: 157 us
  blocking collectives  66.7 us (42%)
  starting transfers between devices  29.7 us (19%)
  waiting for transfers between devices  29.7 us (19%)
  Pallas kernels  26.5 us (17%)
  local copies, waits for them, and re-layouts  2.87 us (2%)
    all_to_all x1, blocking collectives, on_device(): lax.all_to_all(result, 'exp', split_axis=0, concat_axis=0, tiled=True)  49.8 us
    all_to_all x2, blocking collectives, exchange_y(): lax.all_to_all(x, 'req', split_axis=0, concat_axis=0, tiled=True, axis_in...  16.9 us
    pallas_call x9, Pallas kernels, call(): pl.pallas_call(body, out_shape=out_shape, in_specs=in_specs + [VMEM] * le...  16.5 us
    ppermute x7, waiting for transfers between devices, on_device(): lax.ppermute(packed[d], 'req', [(k, (k + d) % peers) for k in range(peers)])  12.8 us
    all_to_all x1, starting transfers between devices, on_device(): lax.all_to_all(outgoing, 'exp', split_axis=0, concat_axis=0, tiled=True)  11.3 us
    all_to_all x1, waiting for transfers between devices, exchange_y(): lax.all_to_all(x, 'req', split_axis=0, concat_axis=0, tiled=True, axis_in...  8.29 us
    ppermute x6, starting transfers between devices, on_device(): sent += [lax.ppermute(x[d], 'req', along(d)) for x in (gates, ups)]  7.37 us
    ppermute x6, waiting for transfers between devices, on_device(): sent += [lax.ppermute(x[d], 'req', along(d)) for x in (gates, ups)]  6.22 us
  transfers between devices with their start and end apart: 19, of which 10 were waited for; matrix products, arithmetic and copies ran while one was open for 1% of the time, Pallas kernels for 11%

profile of v2, /device:TPU:1, one launch (start us, length us, event | category | flops | bytes accessed | tf_op | source)
XLA Modules:
  0.0 157.2 jit_solution(16909315582115695681)
XLA Ops:
  0.6 1.7 %announce.1 = bf16[4,8,1920]{2,1,0:T(8,128)(2,1)} custom-call(s32[8]{0:T(128)} %refs_0_.1, bf16[8,7168]{1,0:T(8,128)(2,1)} %refs_1_.3, s32[8,8]{1,0:T(8,128)} %refs_2_.1, f32[8,8]{1,0:T(8,128)} %refs_3_.2), custom_call_target="tpu_custom_call" | custom-call | tf_op jit(solution)/shard_map/announce/pallas_call | solution.py:280
  2.4 9.8 %all_to_all.25.refs_0_ = bf16[4,8,1920]{2,1,0:T(8,128)(2,1)S(1)} all-to-all(bf16[4,8,1920]{2,1,0:T(8,128)(2,1)} %announce.1), channel_id=1, replica_groups={{0,64,128,192},{32,96,160,224},{1,65,129,193},{33,97,161,225},{2,66,130..., dimensions={0} | all-to-all | bytes 245760 | tf_op jit(solution)/shard_map/all_to_all | solution.py:323
  12.2 2.2 %route.1 = bf16[32,24,896]{2,1,0:T(8,128)(2,1)} custom-call(bf16[4,8,1920]{2,1,0:T(8,128)(2,1)S(1)} %all_to_all.25.refs_0_), custom_call_target="tpu_custom_call" | custom-call | tf_op jit(solution)/shard_map/route/pallas_call | solution.py:280
  14.4 11.3 %all-to-all-start.1 = ((bf16[32,24,896]{2,1,0:T(8,128)(2,1)}), bf16[32,24,896]{2,1,0:T(8,128)(2,1)}, u32[]{:S(2)}, u32[]{:S(2)}) async-start(bf16[32,24,896]{2,1,0:T(8,128)(2,1)} %route.1), calls=%async_computation.1 | async-start | bytes 2752512 | tf_op jit(solution)/shard_map/all_to_all | solution.py:392
  25.7 2.5 %collective-permute-start.8 = (bf16[896,1024]{1,0:T(8,128)(2,1)}, bf16[896,1024]{1,0:T(8,128)(2,1)}, u32[]{:S(2)}, u32[]{:S(2)}) collective-permute-start(bf16[896,1024]{1,0:T(8,128)(2,1)} %bitcast.9), channel_id=1, source_target_pairs={{0,32},{32,0},{64,96},{96,64},{128,160},{160,128},{192,224},{224,1... | collective-permute-start | bytes 5505032 | tf_op jit(solution)/shard_map/ppermute | solution.py:345
  28.2 0.1 collective-permute-start.9
  28.3 0.0 copy-done
  28.3 0.4 collective-permute-start.16
  28.7 0.1 slice_convert_fusion
  28.8 0.3 dynamic-slice_reduce_fusion.1
  29.1 0.2 collective-permute-start
  29.3 2.3 %collective-permute-done = s32[4]{0:T(128)S(1)} collective-permute-done((s32[4]{0:T(128)S(1)}, s32[4]{0:T(128)S(1)}, u32[]{:S(2)}, u32[]{:S(2)}) %collective-permute-start) | collective-permute-done | bytes 48 | tf_op jit(solution)/shard_map/ppermute | solution.py:353
  31.6 0.1 copy.15
  31.7 0.1 select_n.53
  31.8 0.1 pad_add_fusion
  31.9 0.1 dynamic_slice.7.refs_0_
  32.0 0.9 pack.1
  32.9 0.5 collective-permute-start.1
  33.4 0.0 collective-permute-start.2
  33.4 3.5 %collective-permute-done.1.refs_5_ = bf16[32,1152]{1,0:T(8,128)(2,1)S(1)} collective-permute-done((bf16[32,1152]{1,0:T(8,128)(2,1)S(1)}, bf16[32,1152]{1,0:T(8,128)(2,1)S(1)}, u32[]{:S(2)}, u32[]{:S(2)}) %collective-permute-start.1) | collective-permute-done | bytes 73760 | tf_op jit(solution)/shard_map/ppermute | solution.py:365
  36.8 0.7 collective-permute-start.3
  37.5 0.1 maximum_convert_fusion.refs_2_
  37.6 1.8 %collective-permute-done.2.refs_6_ = bf16[32,1152]{1,0:T(8,128)(2,1)S(1)} collective-permute-done((bf16[32,1152]{1,0:T(8,128)(2,1)S(1)}, bf16[32,1152]{1,0:T(8,128)(2,1)S(1)}, u32[]{:S(2)}, u32[]{:S(2)}) %collective-permute-start.2) | collective-permute-done | bytes 73760 | tf_op jit(solution)/shard_map/ppermute | solution.py:365
  39.3 1.9 %collective-permute-start.4 = (bf16[32,1152]{1,0:T(8,128)(2,1)S(1)}, bf16[32,1152]{1,0:T(8,128)(2,1)S(1)}, u32[]{:S(2)}, u32[]{:S(2)}) collective-permute-start(bf16[32,1152]{1,0:T(8,128)(2,1)S(1)} %get-tuple-element.28), channel_id=1, source_target_pairs={{0,128},{32,160},{64,192},{96,224},{128,0},{160,32},{192,64},{224,... | collective-permute-start | bytes 221192 | tf_op jit(solution)/shard_map/ppermute | solution.py:365
  41.2 1.0 collective-permute-done.3.refs_7_
  42.2 0.9 collective-permute-start.5
  43.1 1.3 collective-permute-done.4.refs_8_
  44.5 0.5 collective-permute-start.6
  44.9 3.0 %collective-permute-done.5.refs_9_ = bf16[32,1152]{1,0:T(8,128)(2,1)S(1)} collective-permute-done((bf16[32,1152]{1,0:T(8,128)(2,1)S(1)}, bf16[32,1152]{1,0:T(8,128)(2,1)S(1)}, u32[]{:S(2)}, u32[]{:S(2)}) %collective-permute-start.5) | collective-permute-done | bytes 73760 | tf_op jit(solution)/shard_map/ppermute | solution.py:365
  47.9 0.0 collective-permute-start.7
  47.9 0.6 pad_add_fusion.1.refs_0_
  48.5 0.5 weigh.1.refs_5_.refs_0_
  49.0 0.7 copy-done.1
  49.7 0.0 collective-permute-done.6.refs_10_
  49.7 2.3 %collective-permute-done.7.refs_11_ = bf16[32,1152]{1,0:T(8,128)(2,1)S(1)} collective-permute-done((bf16[32,1152]{1,0:T(8,128)(2,1)S(1)}, bf16[32,1152]{1,0:T(8,128)(2,1)S(1)}, u32[]{:S(2)}, u32[]{:S(2)}) %collective-permute-start.7) | collective-permute-done | bytes 73760 | tf_op jit(solution)/shard_map/ppermute | solution.py:365
  52.0 5.2 %attend.1 = (bf16[8,36864]{1,0:T(8,128)(2,1)}, bf16[8,32768]{1,0:T(8,128)(2,1)}, f32[8,128]{1,0:T(8,128)S(1)}) custom-call(s32[8]{0:T(128)S(1)} %compare_select_fusion.refs_0_, s32[8]{0:T(128)S(1)} %copy-done.9, f32[8,1152]{1,0:T(8,128)S(1)} %maximum_convert_fusion.refs_2_, bf16[8,36864]{1,0:T(8,128)(2,1)S(1)} %copy-done.4, ...), custom_call_target="tpu_custom_call" | custom-call | tf_op jit(solution)/shard_map/attend/pallas_call | solution.py:280
  57.1 0.6 copy-done.7
  57.7 0.0 collective-permute-done.8.refs_3_
  57.7 0.0 all-to-all-done.1.refs_1_
  57.7 5.3 %gate.1 = (bf16[384,896]{1,0:T(8,128)(2,1)}, bf16[384,896]{1,0:T(8,128)(2,1)}, f32[96,1024]{1,0:T(8,128)}, bf16[96,1024]{1,0:T(8,128)(2,1)}, bf16[96,1024]{1,0:T(8,128)(2,1)}, /*index=5*/bf16[96,1024]{1,0:T(8,128)(2,1)}) custom-call(s32[2]{0:T(128)} %pad_add_fusion.1.refs_0_, bf16[32,24,896]{2,1,0:T(8,128)(2,1)} %all-to-all-done.1.refs_1_, ...), custom_call_target="tpu_custom_call" | custom-call | tf_op jit(solution)/shard_map/gate/pallas_call | solution.py:408
  63.1 0.2 collective-permute-start.10
  63.3 2.1 %collective-permute-start.12 = (bf16[96,1024]{1,0:T(8,128)(2,1)}, bf16[96,1024]{1,0:T(8,128)(2,1)S(1)}, u32[]{:S(2)}, u32[]{:S(2)}) collective-permute-start(bf16[96,1024]{1,0:T(8,128)(2,1)} %get-tuple-element.41), channel_id=1, source_target_pairs={{0,128},{32,160},{64,192},{96,224},{128,0},{160,32},{192,64},{224,... | collective-permute-start | bytes 589832 | tf_op jit(solution)/shard_map/ppermute | solution.py:428
  65.4 0.6 collective-permute-start.14
  66.0 0.0 collective-permute-done.9.up2_ref
  66.0 4.7 %up.1 = (f32[96,1024]{1,0:T(8,128)}, bf16[96,1024]{1,0:T(8,128)(2,1)}, bf16[96,1024]{1,0:T(8,128)(2,1)}, bf16[96,1024]{1,0:T(8,128)(2,1)}) custom-call(bf16[384,896]{1,0:T(8,128)(2,1)} %get-tuple-element.36.own_ref, bf16[384,896]{1,0:T(8,128)(2,1)} %get-tuple-element.37.other_ref, bf16[896,1024]{1,0:T(8,128)(2,1)} %bitcast.12, ...), custom_call_target="tpu_custom_call" | custom-call | tf_op jit(solution)/shard_map/up/pallas_call | solution.py:417
  70.7 0.8 collective-permute-start.11
  71.6 0.0 collective-permute-done.10.refs_2_
  71.6 1.6 %collective-permute-start.13 = (bf16[96,1024]{1,0:T(8,128)(2,1)}, bf16[96,1024]{1,0:T(8,128)(2,1)S(1)}, u32[]{:S(2)}, u32[]{:S(2)}) collective-permute-start(bf16[96,1024]{1,0:T(8,128)(2,1)} %get-tuple-element.42), channel_id=1, source_target_pairs={{0,128},{32,160},{64,192},{96,224},{128,0},{160,32},{192,64},{224,... | collective-permute-start | bytes 589832 | tf_op jit(solution)/shard_map/ppermute | solution.py:428
  73.2 0.0 collective-permute-done.12.refs_4_
  73.2 2.0 %collective-permute-start.15 = (bf16[96,1024]{1,0:T(8,128)(2,1)}, bf16[96,1024]{1,0:T(8,128)(2,1)S(1)}, u32[]{:S(2)}, u32[]{:S(2)}) collective-permute-start(bf16[96,1024]{1,0:T(8,128)(2,1)} %get-tuple-element.44), channel_id=1, source_target_pairs={{0,192},{32,224},{64,0},{96,32},{128,64},{160,96},{192,128},{224,1... | collective-permute-start | bytes 589832 | tf_op jit(solution)/shard_map/ppermute | solution.py:428
  75.1 0.0 collective-permute-done.14.refs_6_
  75.1 5.3 %collective-permute-done.11.refs_3_ = bf16[96,1024]{1,0:T(8,128)(2,1)S(1)} collective-permute-done((bf16[96,1024]{1,0:T(8,128)(2,1)}, bf16[96,1024]{1,0:T(8,128)(2,1)S(1)}, u32[]{:S(2)}, u32[]{:S(2)}) %collective-permute-start.11) | collective-permute-done | bytes 196640 | tf_op jit(solution)/shard_map/ppermute | solution.py:428
  80.4 0.0 collective-permute-done.13.refs_5_
  80.4 0.9 collective-permute-done.15.refs_7_
  81.4 1.0 copy-done.6
  82.4 1.2 units.1
  83.5 3.5 %all-to-all-start.2 = ((bf16[4,96,1024]{2,1,0:T(8,128)(2,1)}), bf16[4,96,1024]{2,1,0:T(8,128)(2,1)S(1)}, u32[]{:S(2)}, u32[]{:S(2)}) async-start(bf16[4,96,1024]{2,1,0:T(8,128)(2,1)} %units.1), calls=%async_computation.2 | async-start | bytes 1572864 | tf_op jit(solution)/shard_map/all_to_all | solution.py:323
  87.0 0.0 collective-permute-done.16.refs_3_
  87.0 8.3 %all-to-all-done.2.refs_1_ = bf16[4,96,1024]{2,1,0:T(8,128)(2,1)S(1)} async-done(((bf16[4,96,1024]{2,1,0:T(8,128)(2,1)}), bf16[4,96,1024]{2,1,0:T(8,128)(2,1)S(1)}, u32[]{:S(2)}, u32[]{:S(2)}) %all-to-all-start.2) | async-done | bytes 786464 | tf_op jit(solution)/shard_map/all_to_all | solution.py:323
  95.3 3.8 %down.1 = bf16[32,24,896]{2,1,0:T(8,128)(2,1)S(1)} custom-call(s32[2]{0:T(128)S(1)} %copy-done.8, bf16[4,96,1024]{2,1,0:T(8,128)(2,1)S(1)} %all-to-all-done.2.refs_1_, bf16[1024,896]{1,0:T(8,128)(2,1)S(1)} %bitcast.8, bf16[1024,896]{1,0:T(8,128)(2,1)} %collective-permute-done.16.refs_3_), custom_call_target="tpu_custom_call" | custom-call | tf_op jit(solution)/shard_map/down/pallas_call | solution.py:280
  99.1 49.8 %all_to_all.26.refs_1_ = bf16[32,24,896]{2,1,0:T(8,128)(2,1)S(1)} all-to-all(bf16[32,24,896]{2,1,0:T(8,128)(2,1)S(1)} %down.1), channel_id=1, replica_groups=mesh['req'=8,'exp'=32] {'exp'}, dimensions={0} | all-to-all | bytes 2752512 | tf_op jit(solution)/shard_map/all_to_all | solution.py:437
  149.0 0.4 combine.1
  149.4 7.1 %all_to_all.27.refs_0_ = bf16[4,8,1792]{2,1,0:T(8,128)(2,1)S(1)} all-to-all(bf16[4,8,1792]{2,1,0:T(8,128)(2,1)S(1)} %combine.1), channel_id=1, replica_groups={{0,64,128,192},{32,96,160,224},{1,65,129,193},{33,97,161,225},{2,66,130..., dimensions={0} | all-to-all | bytes 229376 | tf_op jit(solution)/shard_map/all_to_all | solution.py:323
  156.5 0.7 spread.1
  (22 shorter events, 0.1 us)
Async XLA Ops:
  12.2 16.1 %copy-start = (bf16[1,1024,896]{2,1,0:T(8,128)(2,1)S(1)}, bf16[1,1024,896]{2,1,0:T(8,128)(2,1)}, u32[]{:S(2)}) copy-start(bf16[1,1024,896]{2,1,0:T(8,128)(2,1)} %param.21) | copy-start | bytes 5505028
  12.2 19.8 %copy-start.3 = (bf16[8,36864]{1,0:T(8,128)(2,1)S(1)}, bf16[8,36864]{1,0:T(8,128)(2,1)}, u32[]{:S(2)}) copy-start(bf16[8,36864]{1,0:T(8,128)(2,1)} %refs_1_.4) | copy-start | bytes 1769476
  14.4 23.1 %copy-start.10 = (bf16[8,576]{1,0:T(8,128)(2,1)S(1)}, bf16[8,576]{1,0:T(8,128)(2,1)}, u32[]{:S(2)}) copy-start(bf16[8,576]{1,0:T(8,128)(2,1)} %param.14) | copy-start | bytes 27652
  14.4 28.7 %copy-start.11 = (s32[8]{0:T(128)S(1)}, s32[8]{0:T(128)}, u32[]{:S(2)}) copy-start(s32[8]{0:T(128)} %refs_0_.1) | copy-start | bytes 100
  14.4 37.6 %copy-start.4 = (bf16[8,36864]{1,0:T(8,128)(2,1)S(1)}, bf16[8,36864]{1,0:T(8,128)(2,1)}, u32[]{:S(2)}) copy-start(bf16[8,36864]{1,0:T(8,128)(2,1)} %refs_3_.3) | copy-start | bytes 1769476
  14.4 37.6 %copy-start.9 = (s32[8]{0:T(128)S(1)}, s32[8]{0:T(128)}, u32[]{:S(2)}) copy-start(s32[8]{0:T(128)} %refs_1_.5) | copy-start | bytes 100
  14.4 43.3 %all-to-all-start.1 = ((bf16[32,24,896]{2,1,0:T(8,128)(2,1)}), bf16[32,24,896]{2,1,0:T(8,128)(2,1)}, u32[]{:S(2)}, u32[]{:S(2)}) async-start(bf16[32,24,896]{2,1,0:T(8,128)(2,1)} %route.1), calls=%async_computation.1 | async-start | bytes 2752512 | tf_op jit(solution)/shard_map/all_to_all | solution.py:392
  25.7 32.0 %collective-permute-start.8 = (bf16[896,1024]{1,0:T(8,128)(2,1)}, bf16[896,1024]{1,0:T(8,128)(2,1)}, u32[]{:S(2)}, u32[]{:S(2)}) collective-permute-start(bf16[896,1024]{1,0:T(8,128)(2,1)} %bitcast.9), channel_id=1, source_target_pairs={{0,32},{32,0},{64,96},{96,64},{128,160},{160,128},{192,224},{224,1... | collective-permute-start | bytes 5505032 | tf_op jit(solution)/shard_map/ppermute | solution.py:345
  28.2 37.8 %collective-permute-start.9 = (bf16[896,1024]{1,0:T(8,128)(2,1)}, bf16[896,1024]{1,0:T(8,128)(2,1)}, u32[]{:S(2)}, u32[]{:S(2)}) collective-permute-start(bf16[896,1024]{1,0:T(8,128)(2,1)} %bitcast.11), channel_id=1, source_target_pairs={{0,32},{32,0},{64,96},{96,64},{128,160},{160,128},{192,224},{224,1... | collective-permute-start | bytes 5505032 | tf_op jit(solution)/shard_map/ppermute | solution.py:345
  28.3 58.7 %collective-permute-start.16 = (bf16[1024,896]{1,0:T(8,128)(2,1)S(1)}, bf16[1024,896]{1,0:T(8,128)(2,1)}, u32[]{:S(2)}, u32[]{:S(2)}) collective-permute-start(bf16[1024,896]{1,0:T(8,128)(2,1)S(1)} %bitcast.7), channel_id=1, source_target_pairs={{0,32},{32,0},{64,96},{96,64},{128,160},{160,128},{192,224},{224,1... | collective-permute-start | bytes 5505032 | tf_op jit(solution)/shard_map/ppermute | solution.py:345
  29.1 2.5 %collective-permute-start = (s32[4]{0:T(128)S(1)}, s32[4]{0:T(128)S(1)}, u32[]{:S(2)}, u32[]{:S(2)}) collective-permute-start(s32[4]{0:T(128)S(1)} %get-tuple-element.46), channel_id=1, source_target_pairs={{0,32},{32,0},{64,96},{96,64},{128,160},{160,128},{192,224},{224,1... | collective-permute-start | bytes 56 | tf_op jit(solution)/shard_map/ppermute | solution.py:353
  32.9 4.0 %collective-permute-start.1 = (bf16[32,1152]{1,0:T(8,128)(2,1)S(1)}, bf16[32,1152]{1,0:T(8,128)(2,1)S(1)}, u32[]{:S(2)}, u32[]{:S(2)}) collective-permute-start(bf16[32,1152]{1,0:T(8,128)(2,1)S(1)} %get-tuple-element.25), channel_id=1, source_target_pairs={{0,32},{32,64},{64,96},{96,128},{128,160},{160,192},{192,224},{224... | collective-permute-start | bytes 221192 | tf_op jit(solution)/shard_map/ppermute | solution.py:365
  33.4 6.0 %collective-permute-start.2 = (bf16[32,1152]{1,0:T(8,128)(2,1)S(1)}, bf16[32,1152]{1,0:T(8,128)(2,1)S(1)}, u32[]{:S(2)}, u32[]{:S(2)}) collective-permute-start(bf16[32,1152]{1,0:T(8,128)(2,1)S(1)} %get-tuple-element.26), channel_id=1, source_target_pairs={{0,64},{32,96},{64,128},{96,160},{128,192},{160,224},{192,0},{224,... | collective-permute-start | bytes 221192 | tf_op jit(solution)/shard_map/ppermute | solution.py:365
  36.8 5.4 %collective-permute-start.3 = (bf16[32,1152]{1,0:T(8,128)(2,1)S(1)}, bf16[32,1152]{1,0:T(8,128)(2,1)S(1)}, u32[]{:S(2)}, u32[]{:S(2)}) collective-permute-start(bf16[32,1152]{1,0:T(8,128)(2,1)S(1)} %get-tuple-element.27), channel_id=1, source_target_pairs={{0,96},{32,128},{64,160},{96,192},{128,224},{160,0},{192,32},{224,... | collective-permute-start | bytes 221192 | tf_op jit(solution)/shard_map/ppermute | solution.py:365
  39.3 5.1 %collective-permute-start.4 = (bf16[32,1152]{1,0:T(8,128)(2,1)S(1)}, bf16[32,1152]{1,0:T(8,128)(2,1)S(1)}, u32[]{:S(2)}, u32[]{:S(2)}) collective-permute-start(bf16[32,1152]{1,0:T(8,128)(2,1)S(1)} %get-tuple-element.28), channel_id=1, source_target_pairs={{0,128},{32,160},{64,192},{96,224},{128,0},{160,32},{192,64},{224,... | collective-permute-start | bytes 221192 | tf_op jit(solution)/shard_map/ppermute | solution.py:365
  42.2 5.7 %collective-permute-start.5 = (bf16[32,1152]{1,0:T(8,128)(2,1)S(1)}, bf16[32,1152]{1,0:T(8,128)(2,1)S(1)}, u32[]{:S(2)}, u32[]{:S(2)}) collective-permute-start(bf16[32,1152]{1,0:T(8,128)(2,1)S(1)} %get-tuple-element.29), channel_id=1, source_target_pairs={{0,160},{32,192},{64,224},{96,0},{128,32},{160,64},{192,96},{224,1... | collective-permute-start | bytes 221192 | tf_op jit(solution)/shard_map/ppermute | solution.py:365
  44.5 5.2 %collective-permute-start.6 = (bf16[32,1152]{1,0:T(8,128)(2,1)S(1)}, bf16[32,1152]{1,0:T(8,128)(2,1)S(1)}, u32[]{:S(2)}, u32[]{:S(2)}) collective-permute-start(bf16[32,1152]{1,0:T(8,128)(2,1)S(1)} %get-tuple-element.30), channel_id=1, source_target_pairs={{0,192},{32,224},{64,0},{96,32},{128,64},{160,96},{192,128},{224,1... | collective-permute-start | bytes 221192 | tf_op jit(solution)/shard_map/ppermute | solution.py:365
  47.9 4.1 %collective-permute-start.7 = (bf16[32,1152]{1,0:T(8,128)(2,1)S(1)}, bf16[32,1152]{1,0:T(8,128)(2,1)S(1)}, u32[]{:S(2)}, u32[]{:S(2)}) collective-permute-start(bf16[32,1152]{1,0:T(8,128)(2,1)S(1)} %get-tuple-element.31), channel_id=1, source_target_pairs={{0,224},{32,0},{64,32},{96,64},{128,96},{160,128},{192,160},{224,1... | collective-permute-start | bytes 221192 | tf_op jit(solution)/shard_map/ppermute | solution.py:365
  49.0 0.7 copy-start.1
  57.1 0.6 copy-start.7
  63.1 8.5 %collective-permute-start.10 = (bf16[96,1024]{1,0:T(8,128)(2,1)}, bf16[96,1024]{1,0:T(8,128)(2,1)S(1)}, u32[]{:S(2)}, u32[]{:S(2)}) collective-permute-start(bf16[96,1024]{1,0:T(8,128)(2,1)} %get-tuple-element.39), channel_id=1, source_target_pairs={{0,64},{32,96},{64,128},{96,160},{128,192},{160,224},{192,0},{224,... | collective-permute-start | bytes 589832 | tf_op jit(solution)/shard_map/ppermute | solution.py:428
  63.3 9.8 %collective-permute-start.12 = (bf16[96,1024]{1,0:T(8,128)(2,1)}, bf16[96,1024]{1,0:T(8,128)(2,1)S(1)}, u32[]{:S(2)}, u32[]{:S(2)}) collective-permute-start(bf16[96,1024]{1,0:T(8,128)(2,1)} %get-tuple-element.41), channel_id=1, source_target_pairs={{0,128},{32,160},{64,192},{96,224},{128,0},{160,32},{192,64},{224,... | collective-permute-start | bytes 589832 | tf_op jit(solution)/shard_map/ppermute | solution.py:428
  65.4 9.7 %collective-permute-start.14 = (bf16[96,1024]{1,0:T(8,128)(2,1)}, bf16[96,1024]{1,0:T(8,128)(2,1)S(1)}, u32[]{:S(2)}, u32[]{:S(2)}) collective-permute-start(bf16[96,1024]{1,0:T(8,128)(2,1)} %get-tuple-element.43), channel_id=1, source_target_pairs={{0,192},{32,224},{64,0},{96,32},{128,64},{160,96},{192,128},{224,1... | collective-permute-start | bytes 589832 | tf_op jit(solution)/shard_map/ppermute | solution.py:428
  66.0 15.3 %copy-start.5 = (f32[96,1024]{1,0:T(8,128)S(1)}, f32[96,1024]{1,0:T(8,128)}, u32[]{:S(2)}) copy-start(f32[96,1024]{1,0:T(8,128)} %get-tuple-element.35.refs_0_) | copy-start | bytes 1179652
  70.7 9.7 %collective-permute-start.11 = (bf16[96,1024]{1,0:T(8,128)(2,1)}, bf16[96,1024]{1,0:T(8,128)(2,1)S(1)}, u32[]{:S(2)}, u32[]{:S(2)}) collective-permute-start(bf16[96,1024]{1,0:T(8,128)(2,1)} %get-tuple-element.40), channel_id=1, source_target_pairs={{0,64},{32,96},{64,128},{96,160},{128,192},{160,224},{192,0},{224,... | collective-permute-start | bytes 589832 | tf_op jit(solution)/shard_map/ppermute | solution.py:428
  71.6 8.9 %collective-permute-start.13 = (bf16[96,1024]{1,0:T(8,128)(2,1)}, bf16[96,1024]{1,0:T(8,128)(2,1)S(1)}, u32[]{:S(2)}, u32[]{:S(2)}) collective-permute-start(bf16[96,1024]{1,0:T(8,128)(2,1)} %get-tuple-element.42), channel_id=1, source_target_pairs={{0,128},{32,160},{64,192},{96,224},{128,0},{160,32},{192,64},{224,... | collective-permute-start | bytes 589832 | tf_op jit(solution)/shard_map/ppermute | solution.py:428
  73.2 8.2 %collective-permute-start.15 = (bf16[96,1024]{1,0:T(8,128)(2,1)}, bf16[96,1024]{1,0:T(8,128)(2,1)S(1)}, u32[]{:S(2)}, u32[]{:S(2)}) collective-permute-start(bf16[96,1024]{1,0:T(8,128)(2,1)} %get-tuple-element.44), channel_id=1, source_target_pairs={{0,192},{32,224},{64,0},{96,32},{128,64},{160,96},{192,128},{224,1... | collective-permute-start | bytes 589832 | tf_op jit(solution)/shard_map/ppermute | solution.py:428
  81.4 1.0 copy-start.6
  82.4 13.0 %copy-start.8 = (s32[2]{0:T(128)S(1)}, s32[2]{0:T(128)}, u32[]{:S(2)}) copy-start(s32[2]{0:T(128)} %pad_add_fusion.1.refs_0_) | copy-start | bytes 28
  83.5 11.8 %all-to-all-start.2 = ((bf16[4,96,1024]{2,1,0:T(8,128)(2,1)}), bf16[4,96,1024]{2,1,0:T(8,128)(2,1)S(1)}, u32[]{:S(2)}, u32[]{:S(2)}) async-start(bf16[4,96,1024]{2,1,0:T(8,128)(2,1)} %units.1), calls=%async_computation.2 | async-start | bytes 1572864 | tf_op jit(solution)/shard_map/all_to_all | solution.py:323
  99.1 49.8 %copy-start.2 = (bf16[768,128]{1,0:T(8,128)(2,1)S(1)}, bf16[768,128]{1,0:T(8,128)(2,1)}, u32[]{:S(2)}) copy-start(bf16[768,128]{1,0:T(8,128)(2,1)} %copy-done.1) | copy-start | bytes 589828

commit v3 on v2

--- a/solution.py
+++ b/solution.py
@@ -89,7 +89,7 @@
     place = rank * blocks + (iota((experts, tokens), 1) // rows).astype(F32)
     place = jnp.where(member > 0.5, place, -1.0)
     slots = CAP * blocks
-    row = iota((experts, CORES * slots, tokens), 1)
+    row = iota((1, CORES * slots, tokens), 1)
 
     def slots_of(half, factor):
         wanted = jnp.where(row // slots == half, row % slots, -2).astype(F32)
@@ -402,7 +402,7 @@
     width_own = part // CORES
     column = pl.BlockSpec((width_own, tile), lambda i: (0, i))
     sums_spec = [pl.BlockSpec((size, tile), lambda i: (0, i))] * ring
-    sums_shape = [shape_of((size, inner), F32)] + [shape_of((size, inner))] * (ring - 1)
+    sums_shape = [shape_of((size, inner))] * ring
     rows_spec = [pl.BlockSpec((ring * size, width_own), lambda i: (0, 0))] * 2
     params = pltpu.CompilerParams(vmem_limit_bytes=PART * MIB)
     mine, theirs, *gates = pl.pallas_call(
@@ -424,7 +424,7 @@
         name="up",
     )(mine, theirs, own_weights[1], sibling_weights[1])
     sent = [gates[0], ups[0]]
-    for d in range(1, ring):
+    for d in sorted(range(1, ring), key=lambda d: -min(d, ring - d)):
         sent += [lax.ppermute(x[d], "req", along(d)) for x in (gates, ups)]
     units = call(units_kernel, shape_of((ring, size, inner)), [VMEM] * (2 * ring), "units")(*sent)
     result = call(

time: 160 us -> 160 us (level)
  no operation moved by 1% of the time
where the time goes in v3:
time: 160 us; the launch traced here: 158 us
  blocking collectives  67.1 us (42%)
  starting transfers between devices  31.1 us (19%)
  waiting for transfers between devices  28.7 us (18%)
  Pallas kernels  26.5 us (17%)
  local copies, waits for them, and re-layouts  2.8 us (2%)
    all_to_all x1, blocking collectives, on_device(): lax.all_to_all(result, 'exp', split_axis=0, concat_axis=0, tiled=True)  50.2 us
    all_to_all x2, blocking collectives, exchange_y(): lax.all_to_all(x, 'req', split_axis=0, concat_axis=0, tiled=True, axis_in...  16.9 us
    pallas_call x9, Pallas kernels, call(): pl.pallas_call(body, out_shape=out_shape, in_specs=in_specs + [VMEM] * le...  16.5 us
    ppermute x7, waiting for transfers between devices, on_device(): lax.ppermute(packed[d], 'req', [(k, (k + d) % peers) for k in range(peers)])  12.8 us
    all_to_all x1, starting transfers between devices, on_device(): lax.all_to_all(outgoing, 'exp', split_axis=0, concat_axis=0, tiled=True)  11.3 us
    all_to_all x1, waiting for transfers between devices, exchange_y(): lax.all_to_all(x, 'req', split_axis=0, concat_axis=0, tiled=True, axis_in...  8.35 us
    ppermute x6, starting transfers between devices, on_device(): sent += [lax.ppermute(x[d], 'req', along(d)) for x in (gates, ups)]  7.36 us
    pallas_call x1, Pallas kernels, on_device(): pl.pallas_call(lambda *refs: gate_kernel(*refs[:4], *refs[6:]), grid=(TIL...  5.31 us
  transfers between devices with their start and end apart: 19, of which 10 were waited for; matrix products, arithmetic and copies ran while one was open for 1% of the time, Pallas kernels for 11%

profile of v3, /device:TPU:1, one launch (start us, length us, event | category | flops | bytes accessed | tf_op | source)
XLA Modules:
  0.0 157.8 jit_solution(3831718474721092375)
XLA Ops:
  0.6 1.7 %announce.1 = bf16[4,8,1920]{2,1,0:T(8,128)(2,1)} custom-call(s32[8]{0:T(128)} %refs_0_.1, bf16[8,7168]{1,0:T(8,128)(2,1)} %refs_1_.3, s32[8,8]{1,0:T(8,128)} %refs_2_.1, f32[8,8]{1,0:T(8,128)} %refs_3_.2), custom_call_target="tpu_custom_call" | custom-call | tf_op jit(solution)/shard_map/announce/pallas_call | solution.py:280
  2.4 9.8 %all_to_all.25.refs_0_ = bf16[4,8,1920]{2,1,0:T(8,128)(2,1)S(1)} all-to-all(bf16[4,8,1920]{2,1,0:T(8,128)(2,1)} %announce.1), channel_id=1, replica_groups={{0,64,128,192},{32,96,160,224},{1,65,129,193},{33,97,161,225},{2,66,130..., dimensions={0} | all-to-all | bytes 245760 | tf_op jit(solution)/shard_map/all_to_all | solution.py:323
  12.2 2.2 %route.1 = bf16[32,24,896]{2,1,0:T(8,128)(2,1)} custom-call(bf16[4,8,1920]{2,1,0:T(8,128)(2,1)S(1)} %all_to_all.25.refs_0_), custom_call_target="tpu_custom_call" | custom-call | tf_op jit(solution)/shard_map/route/pallas_call | solution.py:280
  14.4 11.3 %all-to-all-start.1 = ((bf16[32,24,896]{2,1,0:T(8,128)(2,1)}), bf16[32,24,896]{2,1,0:T(8,128)(2,1)}, u32[]{:S(2)}, u32[]{:S(2)}) async-start(bf16[32,24,896]{2,1,0:T(8,128)(2,1)} %route.1), calls=%async_computation.1 | async-start | bytes 2752512 | tf_op jit(solution)/shard_map/all_to_all | solution.py:392
  25.7 2.5 %collective-permute-start.8 = (bf16[896,1024]{1,0:T(8,128)(2,1)}, bf16[896,1024]{1,0:T(8,128)(2,1)}, u32[]{:S(2)}, u32[]{:S(2)}) collective-permute-start(bf16[896,1024]{1,0:T(8,128)(2,1)} %bitcast.9), channel_id=1, source_target_pairs={{0,32},{32,0},{64,96},{96,64},{128,160},{160,128},{192,224},{224,1... | collective-permute-start | bytes 5505032 | tf_op jit(solution)/shard_map/ppermute | solution.py:345
  28.2 0.1 collective-permute-start.9
  28.3 0.0 copy-done
  28.3 0.4 collective-permute-start.16
  28.7 0.1 slice_convert_fusion
  28.8 0.3 dynamic-slice_reduce_fusion.1
  29.1 0.2 collective-permute-start
  29.3 2.3 %collective-permute-done = s32[4]{0:T(128)S(1)} collective-permute-done((s32[4]{0:T(128)S(1)}, s32[4]{0:T(128)S(1)}, u32[]{:S(2)}, u32[]{:S(2)}) %collective-permute-start) | collective-permute-done | bytes 48 | tf_op jit(solution)/shard_map/ppermute | solution.py:353
  31.6 0.1 copy.15
  31.7 0.1 select_n.53
  31.8 0.1 pad_add_fusion
  31.9 0.1 dynamic_slice.7.refs_0_
  32.0 0.9 pack.1
  32.9 0.5 collective-permute-start.1
  33.4 0.0 collective-permute-start.2
  33.4 3.5 %collective-permute-done.1.refs_5_ = bf16[32,1152]{1,0:T(8,128)(2,1)S(1)} collective-permute-done((bf16[32,1152]{1,0:T(8,128)(2,1)S(1)}, bf16[32,1152]{1,0:T(8,128)(2,1)S(1)}, u32[]{:S(2)}, u32[]{:S(2)}) %collective-permute-start.1) | collective-permute-done | bytes 73760 | tf_op jit(solution)/shard_map/ppermute | solution.py:365
  36.8 0.7 collective-permute-start.3
  37.5 0.1 maximum_convert_fusion.refs_2_
  37.6 1.8 %collective-permute-done.2.refs_6_ = bf16[32,1152]{1,0:T(8,128)(2,1)S(1)} collective-permute-done((bf16[32,1152]{1,0:T(8,128)(2,1)S(1)}, bf16[32,1152]{1,0:T(8,128)(2,1)S(1)}, u32[]{:S(2)}, u32[]{:S(2)}) %collective-permute-start.2) | collective-permute-done | bytes 73760 | tf_op jit(solution)/shard_map/ppermute | solution.py:365
  39.3 1.9 %collective-permute-start.4 = (bf16[32,1152]{1,0:T(8,128)(2,1)S(1)}, bf16[32,1152]{1,0:T(8,128)(2,1)S(1)}, u32[]{:S(2)}, u32[]{:S(2)}) collective-permute-start(bf16[32,1152]{1,0:T(8,128)(2,1)S(1)} %get-tuple-element.28), channel_id=1, source_target_pairs={{0,128},{32,160},{64,192},{96,224},{128,0},{160,32},{192,64},{224,... | collective-permute-start | bytes 221192 | tf_op jit(solution)/shard_map/ppermute | solution.py:365
  41.2 1.0 collective-permute-done.3.refs_7_
  42.2 0.9 collective-permute-start.5
  43.1 1.3 collective-permute-done.4.refs_8_
  44.5 0.5 collective-permute-start.6
  44.9 3.0 %collective-permute-done.5.refs_9_ = bf16[32,1152]{1,0:T(8,128)(2,1)S(1)} collective-permute-done((bf16[32,1152]{1,0:T(8,128)(2,1)S(1)}, bf16[32,1152]{1,0:T(8,128)(2,1)S(1)}, u32[]{:S(2)}, u32[]{:S(2)}) %collective-permute-start.5) | collective-permute-done | bytes 73760 | tf_op jit(solution)/shard_map/ppermute | solution.py:365
  47.9 0.0 collective-permute-start.7
  47.9 0.6 pad_add_fusion.1.refs_0_
  48.5 0.5 weigh.1.refs_5_.refs_0_
  49.0 0.7 copy-done.1
  49.7 0.0 collective-permute-done.6.refs_10_
  49.7 2.3 %collective-permute-done.7.refs_11_ = bf16[32,1152]{1,0:T(8,128)(2,1)S(1)} collective-permute-done((bf16[32,1152]{1,0:T(8,128)(2,1)S(1)}, bf16[32,1152]{1,0:T(8,128)(2,1)S(1)}, u32[]{:S(2)}, u32[]{:S(2)}) %collective-permute-start.7) | collective-permute-done | bytes 73760 | tf_op jit(solution)/shard_map/ppermute | solution.py:365
  52.0 5.2 %attend.1 = (bf16[8,36864]{1,0:T(8,128)(2,1)}, bf16[8,32768]{1,0:T(8,128)(2,1)}, f32[8,128]{1,0:T(8,128)S(1)}) custom-call(s32[8]{0:T(128)S(1)} %compare_select_fusion.refs_0_, s32[8]{0:T(128)S(1)} %copy-done.9, f32[8,1152]{1,0:T(8,128)S(1)} %maximum_convert_fusion.refs_2_, bf16[8,36864]{1,0:T(8,128)(2,1)S(1)} %copy-done.4, ...), custom_call_target="tpu_custom_call" | custom-call | tf_op jit(solution)/shard_map/attend/pallas_call | solution.py:280
  57.1 0.6 copy-done.7
  57.7 0.0 collective-permute-done.8.refs_3_
  57.7 0.0 all-to-all-done.1.refs_1_
  57.7 5.3 %gate.1 = (bf16[384,896]{1,0:T(8,128)(2,1)}, bf16[384,896]{1,0:T(8,128)(2,1)}, bf16[96,1024]{1,0:T(8,128)(2,1)}, bf16[96,1024]{1,0:T(8,128)(2,1)}, bf16[96,1024]{1,0:T(8,128)(2,1)}, /*index=5*/bf16[96,1024]{1,0:T(8,128)(2,1)}) custom-call(s32[2]{0:T(128)} %pad_add_fusion.1.refs_0_, bf16[32,24,896]{2,1,0:T(8,128)(2,1)} %all-to-all-done.1.refs_1_, ...), custom_call_target="tpu_custom_call" | custom-call | tf_op jit(solution)/shard_map/gate/pallas_call | solution.py:408
  63.1 0.9 collective-permute-start.10
  64.0 0.8 collective-permute-start.12
  64.8 1.8 %collective-permute-start.14 = (bf16[96,1024]{1,0:T(8,128)(2,1)}, bf16[96,1024]{1,0:T(8,128)(2,1)S(1)}, u32[]{:S(2)}, u32[]{:S(2)}) collective-permute-start(bf16[96,1024]{1,0:T(8,128)(2,1)} %get-tuple-element.43), channel_id=1, source_target_pairs={{0,192},{32,224},{64,0},{96,32},{128,64},{160,96},{192,128},{224,1... | collective-permute-start | bytes 589832 | tf_op jit(solution)/shard_map/ppermute | solution.py:428
  66.6 0.0 collective-permute-done.9.up2_ref
  66.6 4.6 %up.1 = (bf16[96,1024]{1,0:T(8,128)(2,1)}, bf16[96,1024]{1,0:T(8,128)(2,1)}, bf16[96,1024]{1,0:T(8,128)(2,1)}, bf16[96,1024]{1,0:T(8,128)(2,1)}) custom-call(bf16[384,896]{1,0:T(8,128)(2,1)} %get-tuple-element.36.own_ref, bf16[384,896]{1,0:T(8,128)(2,1)} %get-tuple-element.37.other_ref, bf16[896,1024]{1,0:T(8,128)(2,1)} %bitcast.12, ...), custom_call_target="tpu_custom_call" | custom-call | tf_op jit(solution)/shard_map/up/pallas_call | solution.py:417
  71.3 1.1 collective-permute-start.11
  72.4 0.0 collective-permute-done.10.refs_2_
  72.4 0.0 collective-permute-start.13
  72.4 0.0 collective-permute-done.12.refs_4_
  72.4 2.7 %collective-permute-start.15 = (bf16[96,1024]{1,0:T(8,128)(2,1)}, bf16[96,1024]{1,0:T(8,128)(2,1)S(1)}, u32[]{:S(2)}, u32[]{:S(2)}) collective-permute-start(bf16[96,1024]{1,0:T(8,128)(2,1)} %get-tuple-element.44), channel_id=1, source_target_pairs={{0,192},{32,224},{64,0},{96,32},{128,64},{160,96},{192,128},{224,1... | collective-permute-start | bytes 589832 | tf_op jit(solution)/shard_map/ppermute | solution.py:428
  75.1 0.0 collective-permute-done.14.refs_6_
  75.1 3.1 %collective-permute-done.11.refs_3_ = bf16[96,1024]{1,0:T(8,128)(2,1)S(1)} collective-permute-done((bf16[96,1024]{1,0:T(8,128)(2,1)}, bf16[96,1024]{1,0:T(8,128)(2,1)S(1)}, u32[]{:S(2)}, u32[]{:S(2)}) %collective-permute-start.11) | collective-permute-done | bytes 196640 | tf_op jit(solution)/shard_map/ppermute | solution.py:428
  78.2 2.0 %collective-permute-done.13.refs_5_ = bf16[96,1024]{1,0:T(8,128)(2,1)S(1)} collective-permute-done((bf16[96,1024]{1,0:T(8,128)(2,1)}, bf16[96,1024]{1,0:T(8,128)(2,1)S(1)}, u32[]{:S(2)}, u32[]{:S(2)}) %collective-permute-start.13) | collective-permute-done | bytes 196640 | tf_op jit(solution)/shard_map/ppermute | solution.py:428
  80.2 0.0 collective-permute-done.15.refs_7_
  80.2 0.9 copy-done.6
  81.1 1.2 units.1
  82.3 4.9 %all-to-all-start.2 = ((bf16[4,96,1024]{2,1,0:T(8,128)(2,1)}), bf16[4,96,1024]{2,1,0:T(8,128)(2,1)S(1)}, u32[]{:S(2)}, u32[]{:S(2)}) async-start(bf16[4,96,1024]{2,1,0:T(8,128)(2,1)} %units.1), calls=%async_computation.2 | async-start | bytes 1572864 | tf_op jit(solution)/shard_map/all_to_all | solution.py:323
  87.2 0.0 collective-permute-done.16.refs_3_
  87.2 8.4 %all-to-all-done.2.refs_1_ = bf16[4,96,1024]{2,1,0:T(8,128)(2,1)S(1)} async-done(((bf16[4,96,1024]{2,1,0:T(8,128)(2,1)}), bf16[4,96,1024]{2,1,0:T(8,128)(2,1)S(1)}, u32[]{:S(2)}, u32[]{:S(2)}) %all-to-all-start.2) | async-done | bytes 786464 | tf_op jit(solution)/shard_map/all_to_all | solution.py:323
  95.6 3.8 %down.1 = bf16[32,24,896]{2,1,0:T(8,128)(2,1)S(1)} custom-call(s32[2]{0:T(128)S(1)} %copy-done.8, bf16[4,96,1024]{2,1,0:T(8,128)(2,1)S(1)} %all-to-all-done.2.refs_1_, bf16[1024,896]{1,0:T(8,128)(2,1)S(1)} %bitcast.8, bf16[1024,896]{1,0:T(8,128)(2,1)} %collective-permute-done.16.refs_3_), custom_call_target="tpu_custom_call" | custom-call | tf_op jit(solution)/shard_map/down/pallas_call | solution.py:280
  99.4 50.2 %all_to_all.26.refs_1_ = bf16[32,24,896]{2,1,0:T(8,128)(2,1)S(1)} all-to-all(bf16[32,24,896]{2,1,0:T(8,128)(2,1)S(1)} %down.1), channel_id=1, replica_groups=mesh['req'=8,'exp'=32] {'exp'}, dimensions={0} | all-to-all | bytes 2752512 | tf_op jit(solution)/shard_map/all_to_all | solution.py:437
  149.6 0.4 combine.1
  150.0 7.1 %all_to_all.27.refs_0_ = bf16[4,8,1792]{2,1,0:T(8,128)(2,1)S(1)} all-to-all(bf16[4,8,1792]{2,1,0:T(8,128)(2,1)S(1)} %combine.1), channel_id=1, replica_groups={{0,64,128,192},{32,96,160,224},{1,65,129,193},{33,97,161,225},{2,66,130..., dimensions={0} | all-to-all | bytes 229376 | tf_op jit(solution)/shard_map/all_to_all | solution.py:323
  157.1 0.7 spread.1
  (22 shorter events, 0.1 us)
Async XLA Ops:
  12.2 16.1 %copy-start = (bf16[1,1024,896]{2,1,0:T(8,128)(2,1)S(1)}, bf16[1,1024,896]{2,1,0:T(8,128)(2,1)}, u32[]{:S(2)}) copy-start(bf16[1,1024,896]{2,1,0:T(8,128)(2,1)} %param.21) | copy-start | bytes 5505028
  12.2 19.8 %copy-start.3 = (bf16[8,36864]{1,0:T(8,128)(2,1)S(1)}, bf16[8,36864]{1,0:T(8,128)(2,1)}, u32[]{:S(2)}) copy-start(bf16[8,36864]{1,0:T(8,128)(2,1)} %refs_1_.4) | copy-start | bytes 1769476
  14.4 23.1 %copy-start.10 = (bf16[8,576]{1,0:T(8,128)(2,1)S(1)}, bf16[8,576]{1,0:T(8,128)(2,1)}, u32[]{:S(2)}) copy-start(bf16[8,576]{1,0:T(8,128)(2,1)} %param.14) | copy-start | bytes 27652
  14.4 28.7 %copy-start.11 = (s32[8]{0:T(128)S(1)}, s32[8]{0:T(128)}, u32[]{:S(2)}) copy-start(s32[8]{0:T(128)} %refs_0_.1) | copy-start | bytes 100
  14.4 37.6 %copy-start.4 = (bf16[8,36864]{1,0:T(8,128)(2,1)S(1)}, bf16[8,36864]{1,0:T(8,128)(2,1)}, u32[]{:S(2)}) copy-start(bf16[8,36864]{1,0:T(8,128)(2,1)} %refs_3_.3) | copy-start | bytes 1769476
  14.4 37.6 %copy-start.9 = (s32[8]{0:T(128)S(1)}, s32[8]{0:T(128)}, u32[]{:S(2)}) copy-start(s32[8]{0:T(128)} %refs_1_.5) | copy-start | bytes 100
  14.4 43.3 %all-to-all-start.1 = ((bf16[32,24,896]{2,1,0:T(8,128)(2,1)}), bf16[32,24,896]{2,1,0:T(8,128)(2,1)}, u32[]{:S(2)}, u32[]{:S(2)}) async-start(bf16[32,24,896]{2,1,0:T(8,128)(2,1)} %route.1), calls=%async_computation.1 | async-start | bytes 2752512 | tf_op jit(solution)/shard_map/all_to_all | solution.py:392
  25.7 32.0 %collective-permute-start.8 = (bf16[896,1024]{1,0:T(8,128)(2,1)}, bf16[896,1024]{1,0:T(8,128)(2,1)}, u32[]{:S(2)}, u32[]{:S(2)}) collective-permute-start(bf16[896,1024]{1,0:T(8,128)(2,1)} %bitcast.9), channel_id=1, source_target_pairs={{0,32},{32,0},{64,96},{96,64},{128,160},{160,128},{192,224},{224,1... | collective-permute-start | bytes 5505032 | tf_op jit(solution)/shard_map/ppermute | solution.py:345
  28.2 38.4 %collective-permute-start.9 = (bf16[896,1024]{1,0:T(8,128)(2,1)}, bf16[896,1024]{1,0:T(8,128)(2,1)}, u32[]{:S(2)}, u32[]{:S(2)}) collective-permute-start(bf16[896,1024]{1,0:T(8,128)(2,1)} %bitcast.11), channel_id=1, source_target_pairs={{0,32},{32,0},{64,96},{96,64},{128,160},{160,128},{192,224},{224,1... | collective-permute-start | bytes 5505032 | tf_op jit(solution)/shard_map/ppermute | solution.py:345
  28.3 58.9 %collective-permute-start.16 = (bf16[1024,896]{1,0:T(8,128)(2,1)S(1)}, bf16[1024,896]{1,0:T(8,128)(2,1)}, u32[]{:S(2)}, u32[]{:S(2)}) collective-permute-start(bf16[1024,896]{1,0:T(8,128)(2,1)S(1)} %bitcast.7), channel_id=1, source_target_pairs={{0,32},{32,0},{64,96},{96,64},{128,160},{160,128},{192,224},{224,1... | collective-permute-start | bytes 5505032 | tf_op jit(solution)/shard_map/ppermute | solution.py:345
  29.1 2.5 %collective-permute-start = (s32[4]{0:T(128)S(1)}, s32[4]{0:T(128)S(1)}, u32[]{:S(2)}, u32[]{:S(2)}) collective-permute-start(s32[4]{0:T(128)S(1)} %get-tuple-element.46), channel_id=1, source_target_pairs={{0,32},{32,0},{64,96},{96,64},{128,160},{160,128},{192,224},{224,1... | collective-permute-start | bytes 56 | tf_op jit(solution)/shard_map/ppermute | solution.py:353
  32.9 4.0 %collective-permute-start.1 = (bf16[32,1152]{1,0:T(8,128)(2,1)S(1)}, bf16[32,1152]{1,0:T(8,128)(2,1)S(1)}, u32[]{:S(2)}, u32[]{:S(2)}) collective-permute-start(bf16[32,1152]{1,0:T(8,128)(2,1)S(1)} %get-tuple-element.25), channel_id=1, source_target_pairs={{0,32},{32,64},{64,96},{96,128},{128,160},{160,192},{192,224},{224... | collective-permute-start | bytes 221192 | tf_op jit(solution)/shard_map/ppermute | solution.py:365
  33.4 6.0 %collective-permute-start.2 = (bf16[32,1152]{1,0:T(8,128)(2,1)S(1)}, bf16[32,1152]{1,0:T(8,128)(2,1)S(1)}, u32[]{:S(2)}, u32[]{:S(2)}) collective-permute-start(bf16[32,1152]{1,0:T(8,128)(2,1)S(1)} %get-tuple-element.26), channel_id=1, source_target_pairs={{0,64},{32,96},{64,128},{96,160},{128,192},{160,224},{192,0},{224,... | collective-permute-start | bytes 221192 | tf_op jit(solution)/shard_map/ppermute | solution.py:365
  36.8 5.4 %collective-permute-start.3 = (bf16[32,1152]{1,0:T(8,128)(2,1)S(1)}, bf16[32,1152]{1,0:T(8,128)(2,1)S(1)}, u32[]{:S(2)}, u32[]{:S(2)}) collective-permute-start(bf16[32,1152]{1,0:T(8,128)(2,1)S(1)} %get-tuple-element.27), channel_id=1, source_target_pairs={{0,96},{32,128},{64,160},{96,192},{128,224},{160,0},{192,32},{224,... | collective-permute-start | bytes 221192 | tf_op jit(solution)/shard_map/ppermute | solution.py:365
  39.3 5.1 %collective-permute-start.4 = (bf16[32,1152]{1,0:T(8,128)(2,1)S(1)}, bf16[32,1152]{1,0:T(8,128)(2,1)S(1)}, u32[]{:S(2)}, u32[]{:S(2)}) collective-permute-start(bf16[32,1152]{1,0:T(8,128)(2,1)S(1)} %get-tuple-element.28), channel_id=1, source_target_pairs={{0,128},{32,160},{64,192},{96,224},{128,0},{160,32},{192,64},{224,... | collective-permute-start | bytes 221192 | tf_op jit(solution)/shard_map/ppermute | solution.py:365
  42.2 5.7 %collective-permute-start.5 = (bf16[32,1152]{1,0:T(8,128)(2,1)S(1)}, bf16[32,1152]{1,0:T(8,128)(2,1)S(1)}, u32[]{:S(2)}, u32[]{:S(2)}) collective-permute-start(bf16[32,1152]{1,0:T(8,128)(2,1)S(1)} %get-tuple-element.29), channel_id=1, source_target_pairs={{0,160},{32,192},{64,224},{96,0},{128,32},{160,64},{192,96},{224,1... | collective-permute-start | bytes 221192 | tf_op jit(solution)/shard_map/ppermute | solution.py:365
  44.5 5.2 %collective-permute-start.6 = (bf16[32,1152]{1,0:T(8,128)(2,1)S(1)}, bf16[32,1152]{1,0:T(8,128)(2,1)S(1)}, u32[]{:S(2)}, u32[]{:S(2)}) collective-permute-start(bf16[32,1152]{1,0:T(8,128)(2,1)S(1)} %get-tuple-element.30), channel_id=1, source_target_pairs={{0,192},{32,224},{64,0},{96,32},{128,64},{160,96},{192,128},{224,1... | collective-permute-start | bytes 221192 | tf_op jit(solution)/shard_map/ppermute | solution.py:365
  47.9 4.1 %collective-permute-start.7 = (bf16[32,1152]{1,0:T(8,128)(2,1)S(1)}, bf16[32,1152]{1,0:T(8,128)(2,1)S(1)}, u32[]{:S(2)}, u32[]{:S(2)}) collective-permute-start(bf16[32,1152]{1,0:T(8,128)(2,1)S(1)} %get-tuple-element.31), channel_id=1, source_target_pairs={{0,224},{32,0},{64,32},{96,64},{128,96},{160,128},{192,160},{224,1... | collective-permute-start | bytes 221192 | tf_op jit(solution)/shard_map/ppermute | solution.py:365
  49.0 0.7 copy-start.1
  57.1 0.6 copy-start.7
  63.1 9.3 %collective-permute-start.10 = (bf16[96,1024]{1,0:T(8,128)(2,1)}, bf16[96,1024]{1,0:T(8,128)(2,1)S(1)}, u32[]{:S(2)}, u32[]{:S(2)}) collective-permute-start(bf16[96,1024]{1,0:T(8,128)(2,1)} %get-tuple-element.39), channel_id=1, source_target_pairs={{0,128},{32,160},{64,192},{96,224},{128,0},{160,32},{192,64},{224,... | collective-permute-start | bytes 589832 | tf_op jit(solution)/shard_map/ppermute | solution.py:428
  64.0 8.5 %collective-permute-start.12 = (bf16[96,1024]{1,0:T(8,128)(2,1)}, bf16[96,1024]{1,0:T(8,128)(2,1)S(1)}, u32[]{:S(2)}, u32[]{:S(2)}) collective-permute-start(bf16[96,1024]{1,0:T(8,128)(2,1)} %get-tuple-element.41), channel_id=1, source_target_pairs={{0,64},{32,96},{64,128},{96,160},{128,192},{160,224},{192,0},{224,... | collective-permute-start | bytes 589832 | tf_op jit(solution)/shard_map/ppermute | solution.py:428
  64.8 10.3 %collective-permute-start.14 = (bf16[96,1024]{1,0:T(8,128)(2,1)}, bf16[96,1024]{1,0:T(8,128)(2,1)S(1)}, u32[]{:S(2)}, u32[]{:S(2)}) collective-permute-start(bf16[96,1024]{1,0:T(8,128)(2,1)} %get-tuple-element.43), channel_id=1, source_target_pairs={{0,192},{32,224},{64,0},{96,32},{128,64},{160,96},{192,128},{224,1... | collective-permute-start | bytes 589832 | tf_op jit(solution)/shard_map/ppermute | solution.py:428
  66.6 13.6 %copy-start.5 = (bf16[96,1024]{1,0:T(8,128)(2,1)S(1)}, bf16[96,1024]{1,0:T(8,128)(2,1)}, u32[]{:S(2)}) copy-start(bf16[96,1024]{1,0:T(8,128)(2,1)} %get-tuple-element.35.refs_0_) | copy-start | bytes 589828
  71.3 6.9 %collective-permute-start.11 = (bf16[96,1024]{1,0:T(8,128)(2,1)}, bf16[96,1024]{1,0:T(8,128)(2,1)S(1)}, u32[]{:S(2)}, u32[]{:S(2)}) collective-permute-start(bf16[96,1024]{1,0:T(8,128)(2,1)} %get-tuple-element.40), channel_id=1, source_target_pairs={{0,128},{32,160},{64,192},{96,224},{128,0},{160,32},{192,64},{224,... | collective-permute-start | bytes 589832 | tf_op jit(solution)/shard_map/ppermute | solution.py:428
  72.4 7.8 %collective-permute-start.13 = (bf16[96,1024]{1,0:T(8,128)(2,1)}, bf16[96,1024]{1,0:T(8,128)(2,1)S(1)}, u32[]{:S(2)}, u32[]{:S(2)}) collective-permute-start(bf16[96,1024]{1,0:T(8,128)(2,1)} %get-tuple-element.42), channel_id=1, source_target_pairs={{0,64},{32,96},{64,128},{96,160},{128,192},{160,224},{192,0},{224,... | collective-permute-start | bytes 589832 | tf_op jit(solution)/shard_map/ppermute | solution.py:428
  72.4 7.8 %collective-permute-start.15 = (bf16[96,1024]{1,0:T(8,128)(2,1)}, bf16[96,1024]{1,0:T(8,128)(2,1)S(1)}, u32[]{:S(2)}, u32[]{:S(2)}) collective-permute-start(bf16[96,1024]{1,0:T(8,128)(2,1)} %get-tuple-element.44), channel_id=1, source_target_pairs={{0,192},{32,224},{64,0},{96,32},{128,64},{160,96},{192,128},{224,1... | collective-permute-start | bytes 589832 | tf_op jit(solution)/shard_map/ppermute | solution.py:428
  80.2 0.9 copy-start.6
  81.1 14.5 %copy-start.8 = (s32[2]{0:T(128)S(1)}, s32[2]{0:T(128)}, u32[]{:S(2)}) copy-start(s32[2]{0:T(128)} %pad_add_fusion.1.refs_0_) | copy-start | bytes 28
  82.3 13.3 %all-to-all-start.2 = ((bf16[4,96,1024]{2,1,0:T(8,128)(2,1)}), bf16[4,96,1024]{2,1,0:T(8,128)(2,1)S(1)}, u32[]{:S(2)}, u32[]{:S(2)}) async-start(bf16[4,96,1024]{2,1,0:T(8,128)(2,1)} %units.1), calls=%async_computation.2 | async-start | bytes 1572864 | tf_op jit(solution)/shard_map/all_to_all | solution.py:323
  99.4 50.2 %copy-start.2 = (bf16[768,128]{1,0:T(8,128)(2,1)S(1)}, bf16[768,128]{1,0:T(8,128)(2,1)}, u32[]{:S(2)}) copy-start(bf16[768,128]{1,0:T(8,128)(2,1)} %copy-done.1) | copy-start | bytes 589828
